TPU v7x, 128 devices: a whole 4x4x4 slice. The times are simulated.
128 devices in a mesh: prefix: 8 (over z, x_hi), group: 8 (over y, core), tensor: 2 (over x_lo).
Axes of the slice: x: 4 (x_hi: 2, x_lo: 2; x = x_hi * 2 + x_lo), y: 4, z: 4, core: 2. Of those that a mesh axis runs over, the one named last changes fastest.
Arguments:
- resp_query: bfloat16 [1024, 16, 32, 128], P('prefix', 'group', 'tensor'), may hold values from -6 to 6
- response_key: bfloat16 [1024, 16, 4, 128], P('prefix', 'group', 'tensor'), may hold values from -6 to 6
- response_value: bfloat16 [1024, 16, 4, 128], P('prefix', 'group', 'tensor'), may hold values from -6 to 6
- resp_cotangent: bfloat16 [1024, 16, 32, 128], P('prefix', 'group', 'tensor'), may hold values from -300 to 300
- prompt_key: bfloat16 [512, 4, 128], P('prefix', 'tensor'), may hold values from -6.2 to 6.2
- prompt_value_rows: bfloat16 [512, 4, 128], P('prefix', 'tensor'), may hold values from -6 to 6
- key_matrix: bfloat16 [5120, 512], P(None, 'tensor'), may hold values from -0.078125 to 0.078125
- value_matrix: bfloat16 [5120, 512], P(None, 'tensor'), may hold values from -0.078125 to 0.078125
- resp_lengths: int32 [16], replicated, may hold values from 256 to 1024, as said below
Outputs:
- resp_query_grad: bfloat16 [1024, 16, 32, 128], P('prefix', 'group', 'tensor')
- resp_key_grad: bfloat16 [1024, 16, 4, 128], P('prefix', 'group', 'tensor')
- resp_value_grad: bfloat16 [1024, 16, 4, 128], P('prefix', 'group', 'tensor')
- prompt_input_grad: bfloat16 [512, 5120], P('prefix', 'tensor')
Inputs may be any that keep to these rules, and one draw needn't show every extreme that they name: `resp_lengths`: some response has all 1024 tokens and another 1024 // 4 in every draw.
All inputs are finite; a program needn't handle non-finite values.
Results may differ from a plain program's by a relative error of at most 0.0058.
Values may be sent and summed in bfloat16 or wider, within the bound.
No kernel may reach another device: no remote copies, remote signals or barrier semaphores. Data moves between devices by JAX's collectives and lax.ppermute only.
A program may use at most 128 MiB of HBM per device.

v0:
```python
import functools
import math

import jax
import jax.numpy as jnp
from jax import lax
from jax.experimental import pallas as pl
from jax.experimental.pallas import tpu as pltpu
from jax.sharding import PartitionSpec as P

MASKED = -1e30
F32 = jnp.float32
BF16 = jnp.bfloat16


def dot_nt(a, b):
    return lax.dot_general(a, b, (((1,), (1,)), ((), ())), preferred_element_type=F32)


def dot_nn(a, b):
    return lax.dot_general(a, b, (((1,), (0,)), ((), ())), preferred_element_type=F32)


def dot_tn(a, b):
    return lax.dot_general(a, b, (((0,), (0,)), ((), ())), preferred_element_type=F32)


def attention_kernel(tokens, prows, zs, count, meta, *refs):
    refs = list(refs)
    qd_hbm = [[refs.pop(0) for _ in range(2)] for _ in range(count)]
    kv_refs = [refs.pop(0) for _ in range(zs)]
    dq_hbm = [refs.pop(0) for _ in range(2)]
    dkv_hbm = [refs.pop(0) for _ in range(zs)]
    dpkv_hbm = [refs.pop(0) for _ in range(zs)]
    e_ref, dp_ref, m_ref, l_ref, a_ref, mc_ref, dqt_ref, dk_acc, dv_acc = refs[:9]
    qd_refs, dq_refs, dkv_refs, dpkv_ref, in_sem, dq_sem, dkv_sem, dpkv_sem = refs[9:]
    rows, width = qd_refs.shape[3:]

    def incoming(r, half, source=0):
        return pltpu.make_async_copy(qd_hbm[source][half], qd_refs.at[r, half], in_sem.at[r, half])

    def dq_out(r, half):
        return pltpu.make_async_copy(dq_refs.at[r, half], dq_hbm[half].at[r], dq_sem.at[r, half])

    def dkv_out(r, s):
        return pltpu.make_async_copy(dkv_refs.at[r, s], dkv_hbm[s].at[r], dkv_sem.at[r, s])

    def dpkv_out(s):
        return pltpu.make_async_copy(dpkv_ref.at[s], dpkv_hbm[s], dpkv_sem.at[s])

    for r in range(count):
        for half in range(2):
            incoming(r, half, r).start()
    scale = 1.0 / math.sqrt(width)
    log2 = scale * math.log2(math.e)
    z, xh = meta[0], meta[1]
    chunk = 2 * tokens
    pchunk = 4 * prows
    pcount = zs // 2
    pbase = 4 * tokens * count
    prompt_rows = pcount * pchunk

    def prompt_pair(c, which):
        first = pbase + which * 2 * prows
        parts = [kv_refs[2 * c + i][first : first + 2 * prows] for i in range(2)]
        return jnp.concatenate(parts, axis=0)

    def resp_pair(r, s, which):
        first = pl.multiple_of(r * (4 * tokens) + which * chunk, chunk)
        return kv_refs[s][pl.ds(first, chunk)]

    def forward(q, do, keys, values, base, index, mask):
        n = keys.shape[0]
        scores = dot_nt(keys, q)
        if mask is not None:
            scores = jnp.where(mask, scores, MASKED)
        top = jnp.max(scores, axis=0, keepdims=True)
        if index > 0:
            old = m_ref[...]
            top = jnp.maximum(old, top)
        e = jnp.exp2((scores - top) * log2)
        dp = dot_nt(values, do)
        esum = jnp.sum(e, axis=0, keepdims=True)
        dsum = jnp.sum(e * dp, axis=0, keepdims=True)
        if index > 0:
            fix = jnp.exp2((old - top) * log2)
            esum = esum + l_ref[...] * fix
            dsum = dsum + a_ref[...] * fix
        m_ref[...] = top
        l_ref[...] = esum
        a_ref[...] = dsum
        mc_ref[index] = top
        e_ref[base : base + n] = e
        dp_ref[base : base + n] = dp

    def backward(half, q, do, keys, base, index):
        n = keys.shape[0]
        inv = 1.0 / l_ref[...]
        factor = jnp.exp2((mc_ref[index] - m_ref[...]) * log2) * inv
        delta = a_ref[...] * inv
        p = e_ref[base : base + n] * factor
        ds = (p * (dp_ref[base : base + n] - delta)).astype(BF16)
        dv = dot_nn(p.astype(BF16), do)
        dk = dot_nn(ds, q)
        dqt = dot_tn(keys, ds)
        if index == 0:
            dqt_ref[...] = dqt
        else:
            dqt_ref[...] += dqt
        if half == 0 and base >= prompt_rows:
            dk_acc[base : base + n] = dk
            dv_acc[base : base + n] = dv
        else:
            dk_acc[base : base + n] += dk
            dv_acc[base : base + n] += dv

    def when_past(s, step):
        if s == 0:
            step()
        else:
            pl.when(z >= s)(step)

    def one_half(r, half):
        token = lax.rem(lax.broadcasted_iota(jnp.int32, (rows, width), 0), tokens)
        raw = qd_refs[r, half, 1].astype(F32)
        qd_refs[r, half, 1] = jnp.where(token < meta[2 + 2 * r + half], raw, 0.0).astype(BF16)
        q, do = qd_refs[r, half, 0], qd_refs[r, half, 1]
        for c in range(pcount):
            forward(q, do, prompt_pair(c, 0), prompt_pair(c, 1), c * pchunk, c, None)
        for s in range(zs):

            def step(s=s):
                mask = None
                if s == 0:
                    row = lax.broadcasted_iota(jnp.int32, (chunk, rows), 0)
                    lane = lax.broadcasted_iota(jnp.int32, (chunk, rows), 1)
                    slot = row // tokens
                    key_pos = (slot + xh - 2 * slot * xh) * tokens + lax.rem(row, tokens)
                    start = (1 - xh) if half else xh
                    mask = key_pos <= start * tokens + lax.rem(lane, tokens)
                base = pcount * pchunk + s * chunk
                forward(q, do, resp_pair(r, s, 0), resp_pair(r, s, 1), base, pcount + s, mask)

            when_past(s, step)
        for c in range(pcount):
            backward(half, q, do, prompt_pair(c, 0), c * pchunk, c)
        for s in range(zs):

            def step(s=s):
                base = pcount * pchunk + s * chunk
                backward(half, q, do, resp_pair(r, s, 0), base, pcount + s)

            when_past(s, step)
        dq_refs[r, half] = (dqt_ref[...] * scale).T.astype(BF16)

    dk_acc[0:prompt_rows] = jnp.zeros((prompt_rows, width), F32)
    dv_acc[0:prompt_rows] = jnp.zeros((prompt_rows, width), F32)

    @pl.loop(0, count)
    def _(r):
        for half in range(2):
            live = meta[2 + 2 * r + half]
            incoming(r, half).wait()

            @pl.when(live > 0)
            def _(half=half):
                one_half(r, half)

            @pl.when(live <= 0)
            def _(half=half):
                dq_refs[r, half] = jnp.zeros((rows, width), BF16)
                if half == 0:
                    zeros = jnp.zeros((dk_acc.shape[0] - prompt_rows, width), F32)
                    dk_acc[prompt_rows:] = zeros
                    dv_acc[prompt_rows:] = zeros

            dq_out(r, half).start()

        for s in range(zs):

            def store(s=s):
                base = prompt_rows + s * chunk
                dkv_refs[r, s, 0:chunk] = (dk_acc[base : base + chunk] * scale).astype(BF16)
                dkv_refs[r, s, chunk : 2 * chunk] = dv_acc[base : base + chunk].astype(BF16)
                dkv_out(r, s).start()

            when_past(s, store)

    for s in range(zs):
        n = 2 * prows
        span = slice(s * n, (s + 1) * n)
        dpkv_ref[s, 0:n] = (dk_acc[span] * scale).astype(BF16)
        dpkv_ref[s, n : 2 * n] = dv_acc[span].astype(BF16)
        dpkv_out(s).start()
    for s in range(zs):
        dpkv_out(s).wait()
    for r in range(count):
        for half in range(2):
            dq_out(r, half).wait()
        for s in range(zs):
            when_past(s, dkv_out(r, s).wait)


def attention(meta, qds, kvs, count, tokens, prows):
    zs = len(kvs)
    rows, width = qds[0].shape[1:]
    total = zs * 2 * (prows + tokens)
    in_vmem = pl.BlockSpec(memory_space=pltpu.VMEM)
    in_hbm = pl.BlockSpec(memory_space=pltpu.HBM)
    args = [pltpu.with_memory_space_constraint(x, pltpu.HBM) for x in qds] + list(kvs)
    in_specs = [pl.BlockSpec(memory_space=pltpu.SMEM)] + [in_hbm] * len(qds) + [in_vmem] * zs
    out_shape = [pltpu.HBM((count, rows, width), BF16)] * 2
    out_shape += [pltpu.HBM((count, 4 * tokens, width), BF16)] * zs
    out_shape += [pltpu.HBM((4 * prows, width), BF16)] * zs
    scratch = [
        pltpu.VMEM((total, rows), F32),
        pltpu.VMEM((total, rows), F32),
        pltpu.VMEM((1, rows), F32),
        pltpu.VMEM((1, rows), F32),
        pltpu.VMEM((1, rows), F32),
        pltpu.VMEM((zs // 2 + zs, 1, rows), F32),
        pltpu.VMEM((width, rows), F32),
        pltpu.VMEM((total, width), F32),
        pltpu.VMEM((total, width), F32),
        pltpu.VMEM((count, 2, 2, rows, width), BF16),
        pltpu.VMEM((count, 2, rows, width), BF16),
        pltpu.VMEM((count, zs, 4 * tokens, width), BF16),
        pltpu.VMEM((zs, 4 * prows, width), BF16),
        pltpu.SemaphoreType.DMA((count, 2)),
        pltpu.SemaphoreType.DMA((count, 2)),
        pltpu.SemaphoreType.DMA((count, zs)),
        pltpu.SemaphoreType.DMA((zs,)),
    ]
    return pl.pallas_call(
        functools.partial(attention_kernel, tokens, prows, zs, count),
        out_shape=out_shape,
        in_specs=in_specs,
        out_specs=[in_hbm] * len(out_shape),
        scratch_shapes=scratch,
        compiler_params=pltpu.CompilerParams(vmem_limit_bytes=30 * 1024 * 1024),
        cost_estimate=pl.CostEstimate(
            flops=20 * count * rows * total * width,
            bytes_accessed=8 * 1024 * 1024,
            transcendentals=2 * count * rows * total,
        ),
        name="attention_grad",
    )(meta, *args)


def per_device(
    resp_query,
    response_key,
    response_value,
    resp_cotangent,
    prompt_key,
    prompt_value_rows,
    key_matrix,
    value_matrix,
    resp_lengths,
):
    tokens, resp_count, query_heads, width = resp_query.shape
    kv_heads = response_key.shape[2]
    factor = query_heads // kv_heads
    prows = prompt_key.shape[0]
    prefix_size = lax.axis_size("prefix")
    group_size = lax.axis_size("group")
    zs = prefix_size // 2
    prefix = lax.axis_index("prefix")
    z, xh = prefix // 2, prefix % 2
    first = xh == 0

    def swap(x):
        return lax.ppermute(x, "prefix", [(i, i ^ 1) for i in range(prefix_size)])

    def shift(x, s, wrap):
        pairs = [(i, i + 2 * s) for i in range(prefix_size)]
        if wrap:
            pairs = [(i, j % prefix_size) for i, j in pairs]
        else:
            pairs = [(i, j) for i, j in pairs if 0 <= j < prefix_size]
        return lax.ppermute(x, "prefix", pairs)

    def own_away(lo, hi):
        return jnp.where(first, lo, hi), jnp.where(first, hi, lo)

    def in_order(own, other):
        return jnp.where(first, own, other), jnp.where(first, other, own)

    resp = jnp.stack((response_key, response_value), 0).transpose(3, 2, 0, 1, 4)
    prompt = jnp.stack((prompt_key, prompt_value_rows), 0).transpose(2, 0, 1, 3)
    resp_own, resp_away = own_away(resp[0], resp[1])
    prompt_own, prompt_away = own_away(prompt[0], prompt[1])
    flat = jnp.concatenate((resp_away.reshape(-1, width), prompt_away.reshape(-1, width)))
    got = swap(flat)
    split = resp_away.size // width
    resp_got = got[:split].reshape(resp_own.shape)
    prompt_got = got[split:].reshape(prompt_own.shape)
    resp_pair = jnp.stack((resp_own, resp_got), 2).reshape(resp_count, 4 * tokens, width)
    prompt_pair = jnp.stack((prompt_own, prompt_got), 1).reshape(4 * prows, width)

    own_lengths = lax.dynamic_slice_in_dim(
        resp_lengths, lax.axis_index("group") * resp_count, resp_count
    )

    message = jnp.concatenate((resp_pair.reshape(-1, width), prompt_pair))
    kvs = [message] + [shift(message, s, True) for s in range(1, zs)]

    qds = []
    for r in range(resp_count):
        pair = jnp.stack((resp_query[:, r], resp_cotangent[:, r]), 0)
        own, away = own_away(pair[:, :, :factor], pair[:, :, factor:])
        own = own.transpose(0, 2, 1, 3).reshape(2, factor * tokens, width)
        away = away.transpose(0, 2, 1, 3).reshape(2, factor * tokens, width)
        qds += [own, swap(away)]

    live = [
        own_lengths[r] - (2 * z + place) * tokens
        for r in range(resp_count)
        for place in (xh, 1 - xh)
    ]
    meta = jnp.stack([z, xh] + live).astype(jnp.int32)
    outs = list(attention(meta, qds, kvs, resp_count, tokens, prows))
    dq_own, dq_away = outs[:2]
    dkv = outs[2 : 2 + zs]
    dprompt = outs[2 + zs :]

    def exchange(x, step):
        return lax.ppermute(x, "group", [(i, i ^ step) for i in range(group_size)])

    share = dprompt[0].astype(F32)
    for s in range(1, zs):
        share = share + shift(dprompt[s], -s, True).astype(F32)
    dq_got = swap(dq_away)
    share = (share + exchange(share, 1)).astype(BF16)
    terms = [share] + [exchange(share, step) for step in range(2, group_size, 2)]
    terms[1], dkv[1] = lax.optimization_barrier((terms[1], dkv[1]))
    near = shift(dkv[1], -1, False)
    *terms, dq_got = lax.optimization_barrier((*terms, dq_got))
    terms = [x.astype(F32) for x in terms]
    while len(terms) > 1:
        terms = [terms[i] + terms[i + 1] for i in range(0, len(terms), 2)]
    share, *dkv[2:] = lax.optimization_barrier((terms[0].astype(BF16), *dkv[2:]))
    low = share.reshape(2, 2, prows, width)
    low = jnp.concatenate(in_order(low[:, 0], swap(low[:, 1])), 2)
    projected = dot_nt(low[0], key_matrix) + dot_nt(low[1], value_matrix)

    total = dkv[0].astype(F32) + near.astype(F32)
    for s in range(2, zs):
        total = total + shift(dkv[s], -s, False).astype(F32)
    total = total.reshape(resp_count, 2, 2, tokens, width).astype(BF16)
    grads = in_order(total[:, :, 0], swap(total[:, :, 1]))
    grads = jnp.stack(grads, 2).transpose(1, 3, 0, 2, 4)

    tensor = lax.axis_index("tensor")
    half = projected.shape[1] // 2
    mine = lax.dynamic_slice_in_dim(projected, tensor * half, half, 1)
    away = lax.dynamic_slice_in_dim(projected, (1 - tensor) * half, half, 1).astype(BF16)
    away, dq_got = lax.optimization_barrier((away, dq_got))
    pair = [x.reshape(resp_count, factor, tokens, width) for x in in_order(dq_own, dq_got)]
    query_grad = jnp.concatenate(pair, 1).transpose(2, 0, 1, 3)
    got = lax.ppermute(away, "tensor", [(0, 1), (1, 0)])
    prompt_input_grad = (mine + got.astype(F32)).astype(BF16)
    return (query_grad, grads[0], grads[1], prompt_input_grad)


def solution(mesh):
    placed = P("prefix", "group", "tensor", None)
    return jax.shard_map(
        per_device,
        mesh=mesh,
        in_specs=(
            placed,
            placed,
            placed,
            placed,
            P("prefix", "tensor", None),
            P("prefix", "tensor", None),
            P(None, "tensor"),
            P(None, "tensor"),
            P(),
        ),
        out_specs=(placed, placed, placed, P("prefix", "tensor")),
        check_vma=False,
    )
```

profile of v0, /device:TPU:1, one launch (start us, length us, event | category | flops | bytes accessed | tf_op | source)
XLA Modules:
  0.0 106.1 jit_solution(5719303865506015745)
XLA Ops:
  0.7 1.2 %copy_bitcast_fusion = (bf16[1,128,2,2,128]{4,1,0,2,3:T(8,128)(2,1)S(1)}, bf16[1,128,2,2,128]{4,1,0,2,3:T(8,128)(2,1)S(1)}) fusion(bf16[128,2,2,128]{3,2,1,0:T(2,128)(2,1)} %param.11, bf16[128,2,2,128]{3,2,1,0:T(2,128)(2,1)} %param.10), kind=kLoop, calls=%fused_computation.32 | loop fusion | bytes 524288 | tf_op jit(solution)/shard_map/stack | solution.py:289
  1.9 0.9 copy_bitcast_fusion.2
  2.8 3.7 %collective-permute-start.2 = (bf16[640,128]{1,0:T(8,128)(2,1)S(1)}, bf16[640,128]{1,0:T(8,128)(2,1)S(1)}, u32[]{:S(2)}, u32[]{:S(2)}) collective-permute-start(bf16[640,128]{1,0:T(8,128)(2,1)S(1)} %pad_maximum_fusion.4), channel_id=1, source_target_pairs={{0,16},{16,0},{32,48},{48,32},{64,80},{80,64},{96,112},{112,96},{1... | collective-permute-start | bytes 491528 | tf_op jit(solution)/shard_map/ppermute | solution.py:273
  6.5 0.2 slice_bitcast_fusion.1
  6.7 0.2 slice_bitcast_fusion
  6.9 1.5 %select_bitcast_fusion = (bf16[2,8,128,128]{3,1,2,0:T(8,128)(2,1)S(1)}, bf16[2,8,128,128]{3,1,2,0:T(8,128)(2,1)}, bf16[2,8,128,128]{3,1,2,0:T(8,128)(2,1)}, bf16[2,8,128,128]{3,1,2,0:T(8,128)(2,1)S(1)}) fusion(pred[]{:T(512)S(6)} %eq.5, bf16[1,128,16,128]{3,2,1,0:T(8,128)(2,1)S(1)} %get-tuple-element.58, bf16[1,128,16,128]{3,2,1,0:T(8,128)(2,1)S(1)} %get-tuple-element.56, ...), kind=kLoop, calls=%fused_computation.13 | loop fusion | flops 7340032 | bytes 4194305 | tf_op jit(solution)/shard_map/transpose | solution.py:313
  8.3 0.9 copy.31
  9.3 0.9 copy.34
  10.1 2.9 %collective-permute-start.1 = (bf16[2,1024,128]{2,1,0:T(8,128)(2,1)}, bf16[2,1024,128]{2,1,0:T(8,128)(2,1)}, u32[]{:S(2)}, u32[]{:S(2)}) collective-permute-start(bf16[2,1024,128]{2,1,0:T(8,128)(2,1)} %bitcast.19), channel_id=1, source_target_pairs={{0,16},{16,0},{32,48},{48,32},{64,80},{80,64},{96,112},{112,96},{1... | collective-permute-start | bytes 1572872 | tf_op jit(solution)/shard_map/ppermute | solution.py:273
  13.2 1.7 %collective-permute-start.3 = (bf16[1280,128]{1,0:T(8,128)(2,1)S(1)}, bf16[1280,128]{1,0:T(8,128)(2,1)S(1)}, u32[]{:S(2)}, u32[]{:S(2)}) collective-permute-start(bf16[1280,128]{1,0:T(8,128)(2,1)S(1)} %pad_maximum_fusion.2.refs_4_), channel_id=1, source_target_pairs={{0,32},{16,48},{32,64},{48,80},{64,96},{80,112},{96,0},{112,16},{1... | collective-permute-start | bytes 983048 | tf_op jit(solution)/shard_map/ppermute | solution.py:281
  15.0 3.3 %collective-permute-start.4 = (bf16[1280,128]{1,0:T(8,128)(2,1)S(1)}, bf16[1280,128]{1,0:T(8,128)(2,1)}, u32[]{:S(2)}, u32[]{:S(2)}) collective-permute-start(bf16[1280,128]{1,0:T(8,128)(2,1)S(1)} %pad_maximum_fusion.2.refs_4_), channel_id=1, source_target_pairs={{0,64},{16,80},{32,96},{48,112},{64,0},{80,16},{96,32},{112,48},{1... | collective-permute-start | bytes 983048 | tf_op jit(solution)/shard_map/ppermute | solution.py:281
  18.3 0.7 collective-permute-start.5
  19.1 0.6 fusion.11
  22.2 1.9 %copy.30 = bf16[2,8,128,128]{3,2,1,0:T(8,128)(2,1)} copy(bf16[2,8,128,128]{3,1,2,0:T(8,128)(2,1)} %get-tuple-element.74) | data formatting | bytes 1048576 | tf_op jit(solution)/shard_map/transpose | solution.py:312
  24.1 1.9 %copy.33 = bf16[2,8,128,128]{3,2,1,0:T(8,128)(2,1)} copy(bf16[2,8,128,128]{3,1,2,0:T(8,128)(2,1)} %get-tuple-element.55) | data formatting | bytes 1048576 | tf_op jit(solution)/shard_map/transpose | solution.py:312
  26.2 5.4 %collective-permute-done.4.refs_6_ = bf16[1280,128]{1,0:T(8,128)(2,1)} collective-permute-done((bf16[1280,128]{1,0:T(8,128)(2,1)S(1)}, bf16[1280,128]{1,0:T(8,128)(2,1)}, u32[]{:S(2)}, u32[]{:S(2)}) %collective-permute-start.4) | collective-permute-done | bytes 327712 | tf_op jit(solution)/shard_map/ppermute | solution.py:281
  31.6 0.3 collective-permute-done.5.refs_7_
  31.9 2.8 %collective-permute-done.1.refs_3_ = bf16[2,1024,128]{2,1,0:T(8,128)(2,1)} collective-permute-done((bf16[2,1024,128]{2,1,0:T(8,128)(2,1)}, bf16[2,1024,128]{2,1,0:T(8,128)(2,1)}, u32[]{:S(2)}, u32[]{:S(2)}) %collective-permute-start.1) | collective-permute-done | bytes 524320 | tf_op jit(solution)/shard_map/ppermute | solution.py:273
  34.8 13.8 %attention_grad.1 = (bf16[2,1024,128]{2,1,0:T(8,128)(2,1)}, bf16[2,1024,128]{2,1,0:T(8,128)(2,1)}, bf16[2,512,128]{2,1,0:T(8,128)(2,1)}, bf16[2,512,128]{2,1,0:T...) custom-call(s32[6]{0:T(128)S(1)} %stack.68.meta, ...), custom_call_target="tpu_custom_call" | custom-call | flops 8053063680 | bytes 8388608 | tf_op jit(solution)/shard_map/attention_grad/pallas_call | solution.py:234
  48.6 5.3 %collective-permute-start.6 = (bf16[256,128]{1,0:T(8,128)(2,1)}, bf16[256,128]{1,0:T(8,128)(2,1)S(1)}, u32[]{:S(2)}, u32[]{:S(2)}) collective-permute-start(bf16[256,128]{1,0:T(8,128)(2,1)} %get-tuple-element.28), channel_id=1, source_target_pairs={{0,96},{16,112},{32,0},{48,16},{64,32},{80,48},{96,64},{112,80},{1... | collective-permute-start | bytes 196616 | tf_op jit(solution)/shard_map/ppermute | solution.py:281
  53.9 2.5 %collective-permute-start.7 = (bf16[256,128]{1,0:T(8,128)(2,1)}, bf16[256,128]{1,0:T(8,128)(2,1)S(1)}, u32[]{:S(2)}, u32[]{:S(2)}) collective-permute-start(bf16[256,128]{1,0:T(8,128)(2,1)} %get-tuple-element.29), channel_id=1, source_target_pairs={{0,64},{16,80},{32,96},{48,112},{64,0},{80,16},{96,32},{112,48},{1... | collective-permute-start | bytes 196616 | tf_op jit(solution)/shard_map/ppermute | solution.py:281
  56.3 0.9 collective-permute-start.13
  57.2 1.4 %collective-permute-done.7 = bf16[256,128]{1,0:T(8,128)(2,1)S(1)} collective-permute-done((bf16[256,128]{1,0:T(8,128)(2,1)}, bf16[256,128]{1,0:T(8,128)(2,1)S(1)}, u32[]{:S(2)}, u32[]{:S(2)}) %collective-permute-start.7) | collective-permute-done | bytes 65568 | tf_op jit(solution)/shard_map/ppermute | solution.py:281
  58.7 3.8 %collective-permute-done.8 = bf16[256,128]{1,0:T(8,128)(2,1)S(1)} collective-permute-done((bf16[256,128]{1,0:T(8,128)(2,1)}, bf16[256,128]{1,0:T(8,128)(2,1)S(1)}, u32[]{:S(2)}, u32[]{:S(2)}) %collective-permute-start.8) | collective-permute-done | bytes 65568 | tf_op jit(solution)/shard_map/ppermute | solution.py:281
  62.5 0.9 convert_add_fusion
  63.3 0.6 collective-permute-start.9
  63.9 1.0 collective-permute-done.9
  64.9 7.1 %collective-permute-start.10 = (bf16[256,128]{1,0:T(8,128)(2,1)S(1)}, bf16[256,128]{1,0:T(8,128)(2,1)S(1)}, u32[]{:S(2)}, u32[]{:S(2)}) collective-permute-start(bf16[256,128]{1,0:T(8,128)(2,1)S(1)} %add_convert_fusion.3), channel_id=1, source_target_pairs={{0,4},{2,6},{4,0},{6,2},{8,12},{10,14},{12,8},{14,10},{1,5},{3,7},... | collective-permute-start | bytes 196616 | tf_op jit(solution)/shard_map/ppermute | solution.py:328
  72.1 2.5 %collective-permute-start.12 = (bf16[256,128]{1,0:T(8,128)(2,1)S(1)}, bf16[256,128]{1,0:T(8,128)(2,1)S(1)}, u32[]{:S(2)}, u32[]{:S(2)}) collective-permute-start(bf16[256,128]{1,0:T(8,128)(2,1)S(1)} %add_convert_fusion.3), channel_id=1, source_target_pairs={{0,12},{2,14},{4,8},{6,10},{8,4},{10,6},{12,0},{14,2},{1,13},{3,15... | collective-permute-start | bytes 196616 | tf_op jit(solution)/shard_map/ppermute | solution.py:328
  74.5 2.2 %collective-permute-done.11 = bf16[256,128]{1,0:T(8,128)(2,1)S(1)} collective-permute-done((bf16[256,128]{1,0:T(8,128)(2,1)S(1)}, bf16[256,128]{1,0:T(8,128)(2,1)S(1)}, u32[]{:S(2)}, u32[]{:S(2)}) %collective-permute-start.11) | collective-permute-done | bytes 65568 | tf_op jit(solution)/shard_map/ppermute | solution.py:328
  76.8 1.6 %collective-permute-done.12 = bf16[256,128]{1,0:T(8,128)(2,1)S(1)} collective-permute-done((bf16[256,128]{1,0:T(8,128)(2,1)S(1)}, bf16[256,128]{1,0:T(8,128)(2,1)S(1)}, u32[]{:S(2)}, u32[]{:S(2)}) %collective-permute-start.12) | collective-permute-done | bytes 65568 | tf_op jit(solution)/shard_map/ppermute | solution.py:328
  78.4 0.6 collective-permute-start.14
  79.1 1.5 %collective-permute-start.15 = (bf16[2,512,128]{2,1,0:T(8,128)(2,1)}, bf16[2,512,128]{2,1,0:T(8,128)(2,1)S(1)}, u32[]{:S(2)}, u32[]{:S(2)}) collective-permute-start(bf16[2,512,128]{2,1,0:T(8,128)(2,1)} %get-tuple-element.44), channel_id=1, source_target_pairs={{32,0},{48,16},{64,32},{80,48},{96,64},{112,80},{33,1},{49,17},{65... | collective-permute-start | bytes 786440 | tf_op jit(solution)/shard_map/ppermute | solution.py:281
  80.6 1.3 %collective-permute-start.16 = (bf16[2,512,128]{2,1,0:T(8,128)(2,1)}, bf16[2,512,128]{2,1,0:T(8,128)(2,1)S(1)}, u32[]{:S(2)}, u32[]{:S(2)}) collective-permute-start(bf16[2,512,128]{2,1,0:T(8,128)(2,1)} %get-tuple-element.45), channel_id=1, source_target_pairs={{64,0},{80,16},{96,32},{112,48},{65,1},{81,17},{97,33},{113,49},{6... | collective-permute-start | bytes 786440 | tf_op jit(solution)/shard_map/ppermute | solution.py:281
  81.9 1.3 %collective-permute-start.17 = (bf16[2,512,128]{2,1,0:T(8,128)(2,1)}, bf16[2,512,128]{2,1,0:T(8,128)(2,1)S(1)}, u32[]{:S(2)}, u32[]{:S(2)}) collective-permute-start(bf16[2,512,128]{2,1,0:T(8,128)(2,1)} %get-tuple-element.46), channel_id=1, source_target_pairs={{96,0},{112,16},{97,1},{113,17},{98,2},{114,18},{99,3},{115,19},{1... | collective-permute-start | bytes 786440 | tf_op jit(solution)/shard_map/ppermute | solution.py:281
  83.3 0.9 fusion.4
  84.2 0.9 convolution_add_fusion
  85.2 1.0 collective-permute-start.19
  86.2 0.3 copy.42
  86.6 0.3 copy.43
  86.9 1.2 %maximum_bitcast_fusion = bf16[128,2,16,128]{3,2,1,0:T(8,128)(2,1)} fusion(bf16[2,8,128,128]{3,1,0,2:T(8,128)(2,1)S(1)} %copy.43, bf16[2,8,128,128]{3,1,0,2:T(8,128)(2,1)S(1)} %copy.42), kind=kLoop, calls=%fused_computation.5 | loop fusion | flops 2097152 | bytes 2097152 | tf_op jit(solution)/shard_map/transpose | solution.py:360
  88.1 2.8 %collective-permute-done.16 = bf16[2,512,128]{2,1,0:T(8,128)(2,1)S(1)} collective-permute-done((bf16[2,512,128]{2,1,0:T(8,128)(2,1)}, bf16[2,512,128]{2,1,0:T(8,128)(2,1)S(1)}, u32[]{:S(2)}, u32[]{:S(2)}) %collective-permute-start.16) | collective-permute-done | bytes 262176 | tf_op jit(solution)/shard_map/ppermute | solution.py:281
  90.9 7.1 %collective-permute-done.17 = bf16[2,512,128]{2,1,0:T(8,128)(2,1)S(1)} collective-permute-done((bf16[2,512,128]{2,1,0:T(8,128)(2,1)}, bf16[2,512,128]{2,1,0:T(8,128)(2,1)S(1)}, u32[]{:S(2)}, u32[]{:S(2)}) %collective-permute-start.17) | collective-permute-done | bytes 262176 | tf_op jit(solution)/shard_map/ppermute | solution.py:281
  98.2 2.5 %collective-permute-start.18 = (bf16[2,2,128,128]{3,2,1,0:T(8,128)(2,1)S(1)}, bf16[2,2,128,128]{3,2,1,0:T(8,128)(2,1)S(1)}, u32[]{:S(2)}, u32[]{:S(2)}) collective-permute-start(bf16[2,2,128,128]{3,2,1,0:T(8,128)(2,1)S(1)} %slice_bitcast_fusion.6), channel_id=1, source_target_pairs={{0,16},{16,0},{32,48},{48,32},{64,80},{80,64},{96,112},{112,96},{1... | collective-permute-start | bytes 393224 | tf_op jit(solution)/shard_map/ppermute | solution.py:273
  100.7 0.8 add_convert_fusion
  101.5 2.9 %collective-permute-done.18 = bf16[2,2,128,128]{3,2,1,0:T(8,128)(2,1)S(1)} collective-permute-done((bf16[2,2,128,128]{3,2,1,0:T(8,128)(2,1)S(1)}, bf16[2,2,128,128]{3,2,1,0:T(8,128)(2,1)S(1)}, u32[]{:S(2)}, u32[]{:S(2)}) %collective-permute-start.18) | collective-permute-done | bytes 131104 | tf_op jit(solution)/shard_map/ppermute | solution.py:273
  104.5 0.8 copy.46
  105.3 0.8 copy.47
  (51 shorter events, 0.9 us)
Async XLA Ops:
  0.6 82.6 %copy-start = (bf16[5120,256]{1,0:T(8,128)(2,1)S(1)}, bf16[5120,256]{1,0:T(8,128)(2,1)}, u32[]{:S(2)}) copy-start(bf16[5120,256]{1,0:T(8,128)(2,1)} %param.15) | copy-start | bytes 7864324
  0.7 5.8 %copy-start.2 = (bf16[128,2,16,128]{3,2,1,0:T(8,128)(2,1)S(1)}, bf16[128,2,16,128]{3,2,1,0:T(8,128)(2,1)}, u32[]{:S(2)}) copy-start(bf16[128,2,16,128]{3,2,1,0:T(8,128)(2,1)} %param.9) | copy-start | bytes 3145732
  0.7 6.0 %copy-start.3 = (bf16[128,2,16,128]{3,2,1,0:T(8,128)(2,1)S(1)}, bf16[128,2,16,128]{3,2,1,0:T(8,128)(2,1)}, u32[]{:S(2)}) copy-start(bf16[128,2,16,128]{3,2,1,0:T(8,128)(2,1)} %param.12) | copy-start | bytes 3145732
  2.8 10.3 %collective-permute-start.2 = (bf16[640,128]{1,0:T(8,128)(2,1)S(1)}, bf16[640,128]{1,0:T(8,128)(2,1)S(1)}, u32[]{:S(2)}, u32[]{:S(2)}) collective-permute-start(bf16[640,128]{1,0:T(8,128)(2,1)S(1)} %pad_maximum_fusion.4), channel_id=1, source_target_pairs={{0,16},{16,0},{32,48},{48,32},{64,80},{80,64},{96,112},{112,96},{1... | collective-permute-start | bytes 491528 | tf_op jit(solution)/shard_map/ppermute | solution.py:273
  8.3 10.7 %copy-start.6 = (s32[16]{0:T(128)S(1)}, s32[16]{0:T(128)}, u32[]{:S(2)}) copy-start(s32[16]{0:T(128)} %param.17) | copy-start | bytes 196
  9.2 22.7 %collective-permute-start = (bf16[2,1024,128]{2,1,0:T(8,128)(2,1)}, bf16[2,1024,128]{2,1,0:T(8,128)(2,1)}, u32[]{:S(2)}, u32[]{:S(2)}) collective-permute-start(bf16[2,1024,128]{2,1,0:T(8,128)(2,1)} %bitcast.13), channel_id=1, source_target_pairs={{0,16},{16,0},{32,48},{48,32},{64,80},{80,64},{96,112},{112,96},{1... | collective-permute-start | bytes 1572872 | tf_op jit(solution)/shard_map/ppermute | solution.py:273
  10.1 24.6 %collective-permute-start.1 = (bf16[2,1024,128]{2,1,0:T(8,128)(2,1)}, bf16[2,1024,128]{2,1,0:T(8,128)(2,1)}, u32[]{:S(2)}, u32[]{:S(2)}) collective-permute-start(bf16[2,1024,128]{2,1,0:T(8,128)(2,1)} %bitcast.19), channel_id=1, source_target_pairs={{0,16},{16,0},{32,48},{48,32},{64,80},{80,64},{96,112},{112,96},{1... | collective-permute-start | bytes 1572872 | tf_op jit(solution)/shard_map/ppermute | solution.py:273
  13.2 12.9 %collective-permute-start.3 = (bf16[1280,128]{1,0:T(8,128)(2,1)S(1)}, bf16[1280,128]{1,0:T(8,128)(2,1)S(1)}, u32[]{:S(2)}, u32[]{:S(2)}) collective-permute-start(bf16[1280,128]{1,0:T(8,128)(2,1)S(1)} %pad_maximum_fusion.2.refs_4_), channel_id=1, source_target_pairs={{0,32},{16,48},{32,64},{48,80},{64,96},{80,112},{96,0},{112,16},{1... | collective-permute-start | bytes 983048 | tf_op jit(solution)/shard_map/ppermute | solution.py:281
  15.0 16.6 %collective-permute-start.4 = (bf16[1280,128]{1,0:T(8,128)(2,1)S(1)}, bf16[1280,128]{1,0:T(8,128)(2,1)}, u32[]{:S(2)}, u32[]{:S(2)}) collective-permute-start(bf16[1280,128]{1,0:T(8,128)(2,1)S(1)} %pad_maximum_fusion.2.refs_4_), channel_id=1, source_target_pairs={{0,64},{16,80},{32,96},{48,112},{64,0},{80,16},{96,32},{112,48},{1... | collective-permute-start | bytes 983048 | tf_op jit(solution)/shard_map/ppermute | solution.py:281
  18.3 13.7 %collective-permute-start.5 = (bf16[1280,128]{1,0:T(8,128)(2,1)S(1)}, bf16[1280,128]{1,0:T(8,128)(2,1)}, u32[]{:S(2)}, u32[]{:S(2)}) collective-permute-start(bf16[1280,128]{1,0:T(8,128)(2,1)S(1)} %pad_maximum_fusion.2.refs_4_), channel_id=1, source_target_pairs={{0,96},{16,112},{32,0},{48,16},{64,32},{80,48},{96,64},{112,80},{1... | collective-permute-start | bytes 983048 | tf_op jit(solution)/shard_map/ppermute | solution.py:281
  48.6 8.7 %collective-permute-start.6 = (bf16[256,128]{1,0:T(8,128)(2,1)}, bf16[256,128]{1,0:T(8,128)(2,1)S(1)}, u32[]{:S(2)}, u32[]{:S(2)}) collective-permute-start(bf16[256,128]{1,0:T(8,128)(2,1)} %get-tuple-element.28), channel_id=1, source_target_pairs={{0,96},{16,112},{32,0},{48,16},{64,32},{80,48},{96,64},{112,80},{1... | collective-permute-start | bytes 196616 | tf_op jit(solution)/shard_map/ppermute | solution.py:281
  53.9 4.8 %collective-permute-start.7 = (bf16[256,128]{1,0:T(8,128)(2,1)}, bf16[256,128]{1,0:T(8,128)(2,1)S(1)}, u32[]{:S(2)}, u32[]{:S(2)}) collective-permute-start(bf16[256,128]{1,0:T(8,128)(2,1)} %get-tuple-element.29), channel_id=1, source_target_pairs={{0,64},{16,80},{32,96},{48,112},{64,0},{80,16},{96,32},{112,48},{1... | collective-permute-start | bytes 196616 | tf_op jit(solution)/shard_map/ppermute | solution.py:281
  56.3 6.1 %collective-permute-start.8 = (bf16[256,128]{1,0:T(8,128)(2,1)}, bf16[256,128]{1,0:T(8,128)(2,1)S(1)}, u32[]{:S(2)}, u32[]{:S(2)}) collective-permute-start(bf16[256,128]{1,0:T(8,128)(2,1)} %get-tuple-element.30), channel_id=1, source_target_pairs={{0,32},{16,48},{32,64},{48,80},{64,96},{80,112},{96,0},{112,16},{1... | collective-permute-start | bytes 196616 | tf_op jit(solution)/shard_map/ppermute | solution.py:281
  56.3 22.0 %collective-permute-start.13 = (bf16[2,1024,128]{2,1,0:T(8,128)(2,1)}, bf16[2,1024,128]{2,1,0:T(8,128)(2,1)S(1)}, u32[]{:S(2)}, u32[]{:S(2)}) collective-permute-start(bf16[2,1024,128]{2,1,0:T(8,128)(2,1)} %get-tuple-element.33), channel_id=1, source_target_pairs={{0,16},{16,0},{32,48},{48,32},{64,80},{80,64},{96,112},{112,96},{1... | collective-permute-start | bytes 1572872 | tf_op jit(solution)/shard_map/ppermute | solution.py:273
  63.3 1.6 %collective-permute-start.9 = (f32[256,128]{1,0:T(8,128)S(1)}, f32[256,128]{1,0:T(8,128)S(1)}, u32[]{:S(2)}, u32[]{:S(2)}) collective-permute-start(f32[256,128]{1,0:T(8,128)S(1)} %convert_add_fusion), channel_id=1, source_target_pairs={{0,2},{2,0},{4,6},{6,4},{8,10},{10,8},{12,14},{14,12},{1,3},{3,1},... | collective-permute-start | bytes 393224 | tf_op jit(solution)/shard_map/ppermute | solution.py:328
  64.9 9.6 %collective-permute-start.10 = (bf16[256,128]{1,0:T(8,128)(2,1)S(1)}, bf16[256,128]{1,0:T(8,128)(2,1)S(1)}, u32[]{:S(2)}, u32[]{:S(2)}) collective-permute-start(bf16[256,128]{1,0:T(8,128)(2,1)S(1)} %add_convert_fusion.3), channel_id=1, source_target_pairs={{0,4},{2,6},{4,0},{6,2},{8,12},{10,14},{12,8},{14,10},{1,5},{3,7},... | collective-permute-start | bytes 196616 | tf_op jit(solution)/shard_map/ppermute | solution.py:328
  72.1 4.7 %collective-permute-start.11 = (bf16[256,128]{1,0:T(8,128)(2,1)S(1)}, bf16[256,128]{1,0:T(8,128)(2,1)S(1)}, u32[]{:S(2)}, u32[]{:S(2)}) collective-permute-start(bf16[256,128]{1,0:T(8,128)(2,1)S(1)} %add_convert_fusion.3), channel_id=1, source_target_pairs={{0,8},{2,10},{4,12},{6,14},{8,0},{10,2},{12,4},{14,6},{1,9},{3,11}... | collective-permute-start | bytes 196616 | tf_op jit(solution)/shard_map/ppermute | solution.py:328
  72.1 6.3 %collective-permute-start.12 = (bf16[256,128]{1,0:T(8,128)(2,1)S(1)}, bf16[256,128]{1,0:T(8,128)(2,1)S(1)}, u32[]{:S(2)}, u32[]{:S(2)}) collective-permute-start(bf16[256,128]{1,0:T(8,128)(2,1)S(1)} %add_convert_fusion.3), channel_id=1, source_target_pairs={{0,12},{2,14},{4,8},{6,10},{8,4},{10,6},{12,0},{14,2},{1,13},{3,15... | collective-permute-start | bytes 196616 | tf_op jit(solution)/shard_map/ppermute | solution.py:328
  78.4 4.8 %collective-permute-start.14 = (bf16[2,64,128]{2,1,0:T(8,128)(2,1)S(1)}, bf16[2,64,128]{2,1,0:T(8,128)(2,1)S(1)}, u32[]{:S(2)}, u32[]{:S(2)}) collective-permute-start(bf16[2,64,128]{2,1,0:T(8,128)(2,1)S(1)} %slice_bitcast_fusion.8), channel_id=1, source_target_pairs={{0,16},{16,0},{32,48},{48,32},{64,80},{80,64},{96,112},{112,96},{1... | collective-permute-start | bytes 98312 | tf_op jit(solution)/shard_map/ppermute | solution.py:273
  79.1 5.1 %copy-start.1 = (bf16[5120,256]{1,0:T(8,128)(2,1)S(1)}, bf16[5120,256]{1,0:T(8,128)(2,1)}, u32[]{:S(2)}) copy-start(bf16[5120,256]{1,0:T(8,128)(2,1)} %param.16) | copy-start | bytes 7864324
  79.1 9.1 %collective-permute-start.15 = (bf16[2,512,128]{2,1,0:T(8,128)(2,1)}, bf16[2,512,128]{2,1,0:T(8,128)(2,1)S(1)}, u32[]{:S(2)}, u32[]{:S(2)}) collective-permute-start(bf16[2,512,128]{2,1,0:T(8,128)(2,1)} %get-tuple-element.44), channel_id=1, source_target_pairs={{32,0},{48,16},{64,32},{80,48},{96,64},{112,80},{33,1},{49,17},{65... | collective-permute-start | bytes 786440 | tf_op jit(solution)/shard_map/ppermute | solution.py:281
  80.6 10.3 %collective-permute-start.16 = (bf16[2,512,128]{2,1,0:T(8,128)(2,1)}, bf16[2,512,128]{2,1,0:T(8,128)(2,1)S(1)}, u32[]{:S(2)}, u32[]{:S(2)}) collective-permute-start(bf16[2,512,128]{2,1,0:T(8,128)(2,1)} %get-tuple-element.45), channel_id=1, source_target_pairs={{64,0},{80,16},{96,32},{112,48},{65,1},{81,17},{97,33},{113,49},{6... | collective-permute-start | bytes 786440 | tf_op jit(solution)/shard_map/ppermute | solution.py:281
  81.9 16.2 %collective-permute-start.17 = (bf16[2,512,128]{2,1,0:T(8,128)(2,1)}, bf16[2,512,128]{2,1,0:T(8,128)(2,1)S(1)}, u32[]{:S(2)}, u32[]{:S(2)}) collective-permute-start(bf16[2,512,128]{2,1,0:T(8,128)(2,1)} %get-tuple-element.46), channel_id=1, source_target_pairs={{96,0},{112,16},{97,1},{113,17},{98,2},{114,18},{99,3},{115,19},{1... | collective-permute-start | bytes 786440 | tf_op jit(solution)/shard_map/ppermute | solution.py:281
  84.2 1.9 %copy-start.4 = (bf16[2,1024,128]{2,1,0:T(8,128)(2,1)S(1)}, bf16[2,1024,128]{2,1,0:T(8,128)(2,1)}, u32[]{:S(2)}) copy-start(bf16[2,1024,128]{2,1,0:T(8,128)(2,1)} %get-tuple-element.26) | copy-start | bytes 1572868
  85.2 15.6 %collective-permute-start.19 = (bf16[64,2560]{1,0:T(8,128)(2,1)S(1)}, bf16[64,2560]{1,0:T(8,128)(2,1)S(1)}, u32[]{:S(2)}, u32[]{:S(2)}) collective-permute-start(bf16[64,2560]{1,0:T(8,128)(2,1)S(1)} %dynamic-slice_convert_fusion), channel_id=1, source_target_pairs={{0,1},{1,0},{2,3},{3,2},{4,5},{5,4},{6,7},{7,6},{8,9},{9,8},{10,11... | collective-permute-start | bytes 983048 | tf_op jit(solution)/shard_map/ppermute | solution.py:361
  86.2 11.9 %copy-start.5 = (bf16[2,512,128]{2,1,0:T(8,128)(2,1)S(1)}, bf16[2,512,128]{2,1,0:T(8,128)(2,1)}, u32[]{:S(2)}) copy-start(bf16[2,512,128]{2,1,0:T(8,128)(2,1)} %get-tuple-element.43) | copy-start | bytes 786436
  98.2 6.2 %collective-permute-start.18 = (bf16[2,2,128,128]{3,2,1,0:T(8,128)(2,1)S(1)}, bf16[2,2,128,128]{3,2,1,0:T(8,128)(2,1)S(1)}, u32[]{:S(2)}, u32[]{:S(2)}) collective-permute-start(bf16[2,2,128,128]{3,2,1,0:T(8,128)(2,1)S(1)} %slice_bitcast_fusion.6), channel_id=1, source_target_pairs={{0,16},{16,0},{32,48},{48,32},{64,80},{80,64},{96,112},{112,96},{1... | collective-permute-start | bytes 393224 | tf_op jit(solution)/shard_map/ppermute | solution.py:273
where the time goes:
time: 108 us; the launch traced here: 106 us
  starting transfers between devices  39.4 us (36%)
  waiting for transfers between devices  31.5 us (29%)
  Pallas kernels  13.8 us (13%)
  local copies, waits for them, and re-layouts  11.2 us (10%)
  other arithmetic  4.75 us (4%)
  between operations  3.54 us (3%)
  matrix products  1.82 us (2%)
    ppermute x9, waiting for transfers between devices, shift(): return lax.ppermute(x, 'prefix', pairs)  21 us
    ppermute x9, starting transfers between devices, shift(): return lax.ppermute(x, 'prefix', pairs)  17.6 us
    pallas_call x1, Pallas kernels, attention(): pl.pallas_call(functools.partial(attention_kernel, tokens, prows, zs, cou...  13.8 us
    ppermute x6, starting transfers between devices, swap(): return lax.ppermute(x, 'prefix', [(i, i ^ 1) for i in range(prefix_size)])  10.7 us
    ppermute x4, starting transfers between devices, exchange(): return lax.ppermute(x, 'group', [(i, i ^ step) for i in range(group_size)])  10.2 us
    ppermute x6, waiting for transfers between devices, swap(): return lax.ppermute(x, 'prefix', [(i, i ^ 1) for i in range(prefix_size)])  5.72 us
    ppermute x4, waiting for transfers between devices, exchange(): return lax.ppermute(x, 'group', [(i, i ^ step) for i in range(group_size)])  4.82 us
    transpose x2, local copies, waits for them, and re-layouts, per_device(): own = own.transpose(0, 2, 1, 3).reshape(2, factor * tokens, width)  3.88 us
  transfers between devices with their start and end apart: 20, of which 12 were waited for; matrix products, arithmetic and copies ran while one was open for 13% of the time, Pallas kernels for 0%

commit v1 on v0

--- a/solution.py
+++ b/solution.py
@@ -120,37 +120,43 @@
         else:
             pl.when(z >= s)(step)
 
+    def past_all(step):
+        @pl.when(z == zs - 1)
+        def _():
+            for s in range(zs):
+                step(s)
+
+        @pl.when(z < zs - 1)
+        def _():
+            for s in range(zs):
+                when_past(s, functools.partial(step, s))
+
     def one_half(r, half):
-        token = lax.rem(lax.broadcasted_iota(jnp.int32, (rows, width), 0), tokens)
+        token = lax.broadcasted_iota(jnp.int32, (rows, width), 0) & (tokens - 1)
         raw = qd_refs[r, half, 1].astype(F32)
         qd_refs[r, half, 1] = jnp.where(token < meta[2 + 2 * r + half], raw, 0.0).astype(BF16)
         q, do = qd_refs[r, half, 0], qd_refs[r, half, 1]
         for c in range(pcount):
             forward(q, do, prompt_pair(c, 0), prompt_pair(c, 1), c * pchunk, c, None)
-        for s in range(zs):
-
-            def step(s=s):
-                mask = None
-                if s == 0:
-                    row = lax.broadcasted_iota(jnp.int32, (chunk, rows), 0)
-                    lane = lax.broadcasted_iota(jnp.int32, (chunk, rows), 1)
-                    slot = row // tokens
-                    key_pos = (slot + xh - 2 * slot * xh) * tokens + lax.rem(row, tokens)
-                    start = (1 - xh) if half else xh
-                    mask = key_pos <= start * tokens + lax.rem(lane, tokens)
-                base = pcount * pchunk + s * chunk
-                forward(q, do, resp_pair(r, s, 0), resp_pair(r, s, 1), base, pcount + s, mask)
-
-            when_past(s, step)
+        def forward_step(s):
+            mask = None
+            if s == 0:
+                row = lax.broadcasted_iota(jnp.int32, (chunk, rows), 0)
+                lane = lax.broadcasted_iota(jnp.int32, (1, rows), 1)
+                start = (1 - xh) if half else xh
+                token = (lane & (tokens - 1)) + start * tokens
+                mask = (row ^ (xh * tokens)) <= token
+            base = pcount * pchunk + s * chunk
+            forward(q, do, resp_pair(r, s, 0), resp_pair(r, s, 1), base, pcount + s, mask)
+
+        past_all(forward_step)
         for c in range(pcount):
             backward(half, q, do, prompt_pair(c, 0), c * pchunk, c)
-        for s in range(zs):
-
-            def step(s=s):
-                base = pcount * pchunk + s * chunk
-                backward(half, q, do, resp_pair(r, s, 0), base, pcount + s)
-
-            when_past(s, step)
+        def backward_step(s):
+            base = pcount * pchunk + s * chunk
+            backward(half, q, do, resp_pair(r, s, 0), base, pcount + s)
+
+        past_all(backward_step)
         dq_refs[r, half] = (dqt_ref[...] * scale).T.astype(BF16)
 
     dk_acc[0:prompt_rows] = jnp.zeros((prompt_rows, width), F32)

time: 108 us -> 108 us (level); the launches traced: 106 us -> 108 us
  starting transfers between devices: 39.4 us -> 41.7 us
  waiting for transfers between devices: 31.5 us -> 29.7 us
  Pallas kernels: 13.8 us -> 15.1 us
    ppermute x9, starting transfers between devices: 17.6 us -> 22.8 us  [shift(): return lax.ppermute(x, 'prefix', pairs)]
    ppermute x4, starting transfers between devices: 10.2 us -> 7.27 us  [exchange(): return lax.ppermute(x, 'group', [(i, i ^ step) for i in range(group_size)])]
    ppermute x9, waiting for transfers between devices: 21 us -> 18.7 us  [shift(): return lax.ppermute(x, 'prefix', pairs)]
    pallas_call x1, Pallas kernels: 13.8 us -> 15.1 us  [attention(): pl.pallas_call(functools.partial(attention_kernel, tokens, prows, zs, cou...]
  transfers between devices with their start and end apart: 20 -> 20, of which waited for: 12 -> 11; matrix products, arithmetic and copies ran while one was open for 13% -> 13% of each run, Pallas kernels for 0% -> 0%
where the time goes in v1:
time: 108 us
  starting transfers between devices  41.7 us (39%)
  waiting for transfers between devices  29.7 us (28%)
  Pallas kernels  15.1 us (14%)
  local copies, waits for them, and re-layouts  11.2 us (10%)
  other arithmetic  4.75 us (4%)
  between operations  3.54 us (3%)
  matrix products  1.82 us (2%)
    ppermute x9, starting transfers between devices, shift(): return lax.ppermute(x, 'prefix', pairs)  22.8 us
    ppermute x9, waiting for transfers between devices, shift(): return lax.ppermute(x, 'prefix', pairs)  18.7 us
    pallas_call x1, Pallas kernels, attention(): pl.pallas_call(functools.partial(attention_kernel, tokens, prows, zs, cou...  15.1 us
    ppermute x6, starting transfers between devices, swap(): return lax.ppermute(x, 'prefix', [(i, i ^ 1) for i in range(prefix_size)])  10.6 us
    ppermute x4, starting transfers between devices, exchange(): return lax.ppermute(x, 'group', [(i, i ^ step) for i in range(group_size)])  7.27 us
    ppermute x6, waiting for transfers between devices, swap(): return lax.ppermute(x, 'prefix', [(i, i ^ 1) for i in range(prefix_size)])  5.65 us
    ppermute x4, waiting for transfers between devices, exchange(): return lax.ppermute(x, 'group', [(i, i ^ step) for i in range(group_size)])  5.44 us
    transpose x2, local copies, waits for them, and re-layouts, per_device(): own = own.transpose(0, 2, 1, 3).reshape(2, factor * tokens, width)  3.88 us
  transfers between devices with their start and end apart: 20, of which 11 were waited for; matrix products, arithmetic and copies ran while one was open for 13% of the time, Pallas kernels for 0%

profile of v1, /device:TPU:1, one launch (start us, length us, event | category | flops | bytes accessed | tf_op | source)
XLA Modules:
  0.0 107.8 jit_solution(4720827732182322422)
XLA Ops:
  0.7 1.2 %copy_bitcast_fusion = (bf16[1,128,2,2,128]{4,1,0,2,3:T(8,128)(2,1)S(1)}, bf16[1,128,2,2,128]{4,1,0,2,3:T(8,128)(2,1)S(1)}) fusion(bf16[128,2,2,128]{3,2,1,0:T(2,128)(2,1)} %param.11, bf16[128,2,2,128]{3,2,1,0:T(2,128)(2,1)} %param.10), kind=kLoop, calls=%fused_computation.32 | loop fusion | bytes 524288 | tf_op jit(solution)/shard_map/stack | solution.py:295
  1.9 0.9 copy_bitcast_fusion.2
  2.8 3.7 %collective-permute-start.2 = (bf16[640,128]{1,0:T(8,128)(2,1)S(1)}, bf16[640,128]{1,0:T(8,128)(2,1)S(1)}, u32[]{:S(2)}, u32[]{:S(2)}) collective-permute-start(bf16[640,128]{1,0:T(8,128)(2,1)S(1)} %pad_maximum_fusion.4), channel_id=1, source_target_pairs={{0,16},{16,0},{32,48},{48,32},{64,80},{80,64},{96,112},{112,96},{1... | collective-permute-start | bytes 491528 | tf_op jit(solution)/shard_map/ppermute | solution.py:279
  6.7 0.2 slice_bitcast_fusion
  6.9 1.5 %select_bitcast_fusion = (bf16[2,8,128,128]{3,1,2,0:T(8,128)(2,1)S(1)}, bf16[2,8,128,128]{3,1,2,0:T(8,128)(2,1)}, bf16[2,8,128,128]{3,1,2,0:T(8,128)(2,1)}, bf16[2,8,128,128]{3,1,2,0:T(8,128)(2,1)S(1)}) fusion(pred[]{:T(512)S(6)} %eq.5, bf16[1,128,16,128]{3,2,1,0:T(8,128)(2,1)S(1)} %get-tuple-element.58, bf16[1,128,16,128]{3,2,1,0:T(8,128)(2,1)S(1)} %get-tuple-element.56, ...), kind=kLoop, calls=%fused_computation.13 | loop fusion | flops 7340032 | bytes 4194305 | tf_op jit(solution)/shard_map/transpose | solution.py:319
  8.3 0.9 copy.31
  9.3 0.9 copy.34
  10.1 2.9 %collective-permute-start.1 = (bf16[2,1024,128]{2,1,0:T(8,128)(2,1)}, bf16[2,1024,128]{2,1,0:T(8,128)(2,1)}, u32[]{:S(2)}, u32[]{:S(2)}) collective-permute-start(bf16[2,1024,128]{2,1,0:T(8,128)(2,1)} %bitcast.19), channel_id=1, source_target_pairs={{0,16},{16,0},{32,48},{48,32},{64,80},{80,64},{96,112},{112,96},{1... | collective-permute-start | bytes 1572872 | tf_op jit(solution)/shard_map/ppermute | solution.py:279
  13.2 1.7 %collective-permute-start.3 = (bf16[1280,128]{1,0:T(8,128)(2,1)S(1)}, bf16[1280,128]{1,0:T(8,128)(2,1)S(1)}, u32[]{:S(2)}, u32[]{:S(2)}) collective-permute-start(bf16[1280,128]{1,0:T(8,128)(2,1)S(1)} %pad_maximum_fusion.2.refs_4_), channel_id=1, source_target_pairs={{0,32},{16,48},{32,64},{48,80},{64,96},{80,112},{96,0},{112,16},{1... | collective-permute-start | bytes 983048 | tf_op jit(solution)/shard_map/ppermute | solution.py:287
  15.0 3.3 %collective-permute-start.4 = (bf16[1280,128]{1,0:T(8,128)(2,1)S(1)}, bf16[1280,128]{1,0:T(8,128)(2,1)}, u32[]{:S(2)}, u32[]{:S(2)}) collective-permute-start(bf16[1280,128]{1,0:T(8,128)(2,1)S(1)} %pad_maximum_fusion.2.refs_4_), channel_id=1, source_target_pairs={{0,64},{16,80},{32,96},{48,112},{64,0},{80,16},{96,32},{112,48},{1... | collective-permute-start | bytes 983048 | tf_op jit(solution)/shard_map/ppermute | solution.py:287
  18.3 0.7 collective-permute-start.5
  19.1 0.6 fusion.11
  22.2 1.9 %copy.30 = bf16[2,8,128,128]{3,2,1,0:T(8,128)(2,1)} copy(bf16[2,8,128,128]{3,1,2,0:T(8,128)(2,1)} %get-tuple-element.74) | data formatting | bytes 1048576 | tf_op jit(solution)/shard_map/transpose | solution.py:318
  24.1 1.9 %copy.33 = bf16[2,8,128,128]{3,2,1,0:T(8,128)(2,1)} copy(bf16[2,8,128,128]{3,1,2,0:T(8,128)(2,1)} %get-tuple-element.55) | data formatting | bytes 1048576 | tf_op jit(solution)/shard_map/transpose | solution.py:318
  26.2 5.4 %collective-permute-done.4.refs_6_ = bf16[1280,128]{1,0:T(8,128)(2,1)} collective-permute-done((bf16[1280,128]{1,0:T(8,128)(2,1)S(1)}, bf16[1280,128]{1,0:T(8,128)(2,1)}, u32[]{:S(2)}, u32[]{:S(2)}) %collective-permute-start.4) | collective-permute-done | bytes 327712 | tf_op jit(solution)/shard_map/ppermute | solution.py:287
  31.6 0.3 collective-permute-done.5.refs_7_
  31.9 2.8 %collective-permute-done.1.refs_3_ = bf16[2,1024,128]{2,1,0:T(8,128)(2,1)} collective-permute-done((bf16[2,1024,128]{2,1,0:T(8,128)(2,1)}, bf16[2,1024,128]{2,1,0:T(8,128)(2,1)}, u32[]{:S(2)}, u32[]{:S(2)}) %collective-permute-start.1) | collective-permute-done | bytes 524320 | tf_op jit(solution)/shard_map/ppermute | solution.py:279
  34.8 15.1 %attention_grad.1 = (bf16[2,1024,128]{2,1,0:T(8,128)(2,1)}, bf16[2,1024,128]{2,1,0:T(8,128)(2,1)}, bf16[2,512,128]{2,1,0:T(8,128)(2,1)}, bf16[2,512,128]{2,1,0:T...) custom-call(s32[6]{0:T(128)S(1)} %stack.68.meta, ...), custom_call_target="tpu_custom_call" | custom-call | flops 8053063680 | bytes 8388608 | tf_op jit(solution)/shard_map/attention_grad/pallas_call | solution.py:240
  49.9 7.1 %collective-permute-start.6 = (bf16[256,128]{1,0:T(8,128)(2,1)}, bf16[256,128]{1,0:T(8,128)(2,1)S(1)}, u32[]{:S(2)}, u32[]{:S(2)}) collective-permute-start(bf16[256,128]{1,0:T(8,128)(2,1)} %get-tuple-element.28), channel_id=1, source_target_pairs={{0,96},{16,112},{32,0},{48,16},{64,32},{80,48},{96,64},{112,80},{1... | collective-permute-start | bytes 196616 | tf_op jit(solution)/shard_map/ppermute | solution.py:287
  57.0 5.0 %collective-permute-start.7 = (bf16[256,128]{1,0:T(8,128)(2,1)}, bf16[256,128]{1,0:T(8,128)(2,1)S(1)}, u32[]{:S(2)}, u32[]{:S(2)}) collective-permute-start(bf16[256,128]{1,0:T(8,128)(2,1)} %get-tuple-element.29), channel_id=1, source_target_pairs={{0,64},{16,80},{32,96},{48,112},{64,0},{80,16},{96,32},{112,48},{1... | collective-permute-start | bytes 196616 | tf_op jit(solution)/shard_map/ppermute | solution.py:287
  62.0 0.8 collective-permute-start.8
  62.8 0.9 collective-permute-start.13
  63.7 0.2 collective-permute-done.7
  63.9 2.8 %collective-permute-done.8 = bf16[256,128]{1,0:T(8,128)(2,1)S(1)} collective-permute-done((bf16[256,128]{1,0:T(8,128)(2,1)}, bf16[256,128]{1,0:T(8,128)(2,1)S(1)}, u32[]{:S(2)}, u32[]{:S(2)}) %collective-permute-start.8) | collective-permute-done | bytes 65568 | tf_op jit(solution)/shard_map/ppermute | solution.py:287
  66.7 0.9 convert_add_fusion
  67.5 3.3 %collective-permute-start.9 = (f32[256,128]{1,0:T(8,128)S(1)}, f32[256,128]{1,0:T(8,128)S(1)}, u32[]{:S(2)}, u32[]{:S(2)}) collective-permute-start(f32[256,128]{1,0:T(8,128)S(1)} %convert_add_fusion), channel_id=1, source_target_pairs={{0,2},{2,0},{4,6},{6,4},{8,10},{10,8},{12,14},{14,12},{1,3},{3,1},... | collective-permute-start | bytes 393224 | tf_op jit(solution)/shard_map/ppermute | solution.py:334
  70.8 1.0 collective-permute-done.9
  71.8 1.4 %collective-permute-start.10 = (bf16[256,128]{1,0:T(8,128)(2,1)S(1)}, bf16[256,128]{1,0:T(8,128)(2,1)S(1)}, u32[]{:S(2)}, u32[]{:S(2)}) collective-permute-start(bf16[256,128]{1,0:T(8,128)(2,1)S(1)} %add_convert_fusion.3), channel_id=1, source_target_pairs={{0,4},{2,6},{4,0},{6,2},{8,12},{10,14},{12,8},{14,10},{1,5},{3,7},... | collective-permute-start | bytes 196616 | tf_op jit(solution)/shard_map/ppermute | solution.py:334
  73.2 2.6 %collective-permute-start.11 = (bf16[256,128]{1,0:T(8,128)(2,1)S(1)}, bf16[256,128]{1,0:T(8,128)(2,1)S(1)}, u32[]{:S(2)}, u32[]{:S(2)}) collective-permute-start(bf16[256,128]{1,0:T(8,128)(2,1)S(1)} %add_convert_fusion.3), channel_id=1, source_target_pairs={{0,8},{2,10},{4,12},{6,14},{8,0},{10,2},{12,4},{14,6},{1,9},{3,11}... | collective-permute-start | bytes 196616 | tf_op jit(solution)/shard_map/ppermute | solution.py:334
  75.8 3.0 %collective-permute-done.11 = bf16[256,128]{1,0:T(8,128)(2,1)S(1)} collective-permute-done((bf16[256,128]{1,0:T(8,128)(2,1)S(1)}, bf16[256,128]{1,0:T(8,128)(2,1)S(1)}, u32[]{:S(2)}, u32[]{:S(2)}) %collective-permute-start.11) | collective-permute-done | bytes 65568 | tf_op jit(solution)/shard_map/ppermute | solution.py:334
  78.8 1.5 %collective-permute-done.12 = bf16[256,128]{1,0:T(8,128)(2,1)S(1)} collective-permute-done((bf16[256,128]{1,0:T(8,128)(2,1)S(1)}, bf16[256,128]{1,0:T(8,128)(2,1)S(1)}, u32[]{:S(2)}, u32[]{:S(2)}) %collective-permute-start.12) | collective-permute-done | bytes 65568 | tf_op jit(solution)/shard_map/ppermute | solution.py:334
  80.3 0.6 collective-permute-start.14
  81.0 1.5 %collective-permute-start.15 = (bf16[2,512,128]{2,1,0:T(8,128)(2,1)}, bf16[2,512,128]{2,1,0:T(8,128)(2,1)S(1)}, u32[]{:S(2)}, u32[]{:S(2)}) collective-permute-start(bf16[2,512,128]{2,1,0:T(8,128)(2,1)} %get-tuple-element.44), channel_id=1, source_target_pairs={{32,0},{48,16},{64,32},{80,48},{96,64},{112,80},{33,1},{49,17},{65... | collective-permute-start | bytes 786440 | tf_op jit(solution)/shard_map/ppermute | solution.py:287
  82.5 1.3 %collective-permute-start.16 = (bf16[2,512,128]{2,1,0:T(8,128)(2,1)}, bf16[2,512,128]{2,1,0:T(8,128)(2,1)S(1)}, u32[]{:S(2)}, u32[]{:S(2)}) collective-permute-start(bf16[2,512,128]{2,1,0:T(8,128)(2,1)} %get-tuple-element.45), channel_id=1, source_target_pairs={{64,0},{80,16},{96,32},{112,48},{65,1},{81,17},{97,33},{113,49},{6... | collective-permute-start | bytes 786440 | tf_op jit(solution)/shard_map/ppermute | solution.py:287
  83.8 1.3 %collective-permute-start.17 = (bf16[2,512,128]{2,1,0:T(8,128)(2,1)}, bf16[2,512,128]{2,1,0:T(8,128)(2,1)S(1)}, u32[]{:S(2)}, u32[]{:S(2)}) collective-permute-start(bf16[2,512,128]{2,1,0:T(8,128)(2,1)} %get-tuple-element.46), channel_id=1, source_target_pairs={{96,0},{112,16},{97,1},{113,17},{98,2},{114,18},{99,3},{115,19},{1... | collective-permute-start | bytes 786440 | tf_op jit(solution)/shard_map/ppermute | solution.py:287
  85.2 0.9 fusion.4
  86.1 0.9 convolution_add_fusion
  87.1 1.0 collective-permute-start.19
  88.1 0.3 copy.42
  88.5 0.3 copy.43
  88.8 1.2 %maximum_bitcast_fusion = bf16[128,2,16,128]{3,2,1,0:T(8,128)(2,1)} fusion(bf16[2,8,128,128]{3,1,0,2:T(8,128)(2,1)S(1)} %copy.43, bf16[2,8,128,128]{3,1,0,2:T(8,128)(2,1)S(1)} %copy.42), kind=kLoop, calls=%fused_computation.5 | loop fusion | flops 2097152 | bytes 2097152 | tf_op jit(solution)/shard_map/transpose | solution.py:366
  90.0 1.7 %collective-permute-done.16 = bf16[2,512,128]{2,1,0:T(8,128)(2,1)S(1)} collective-permute-done((bf16[2,512,128]{2,1,0:T(8,128)(2,1)}, bf16[2,512,128]{2,1,0:T(8,128)(2,1)S(1)}, u32[]{:S(2)}, u32[]{:S(2)}) %collective-permute-start.16) | collective-permute-done | bytes 262176 | tf_op jit(solution)/shard_map/ppermute | solution.py:287
  91.7 8.2 %collective-permute-done.17 = bf16[2,512,128]{2,1,0:T(8,128)(2,1)S(1)} collective-permute-done((bf16[2,512,128]{2,1,0:T(8,128)(2,1)}, bf16[2,512,128]{2,1,0:T(8,128)(2,1)S(1)}, u32[]{:S(2)}, u32[]{:S(2)}) %collective-permute-start.17) | collective-permute-done | bytes 262176 | tf_op jit(solution)/shard_map/ppermute | solution.py:287
  100.1 2.5 %collective-permute-start.18 = (bf16[2,2,128,128]{3,2,1,0:T(8,128)(2,1)S(1)}, bf16[2,2,128,128]{3,2,1,0:T(8,128)(2,1)S(1)}, u32[]{:S(2)}, u32[]{:S(2)}) collective-permute-start(bf16[2,2,128,128]{3,2,1,0:T(8,128)(2,1)S(1)} %slice_bitcast_fusion.6), channel_id=1, source_target_pairs={{0,16},{16,0},{32,48},{48,32},{64,80},{80,64},{96,112},{112,96},{1... | collective-permute-start | bytes 393224 | tf_op jit(solution)/shard_map/ppermute | solution.py:279
  102.6 0.8 add_convert_fusion
  103.4 2.8 %collective-permute-done.18 = bf16[2,2,128,128]{3,2,1,0:T(8,128)(2,1)S(1)} collective-permute-done((bf16[2,2,128,128]{3,2,1,0:T(8,128)(2,1)S(1)}, bf16[2,2,128,128]{3,2,1,0:T(8,128)(2,1)S(1)}, u32[]{:S(2)}, u32[]{:S(2)}) %collective-permute-start.18) | collective-permute-done | bytes 131104 | tf_op jit(solution)/shard_map/ppermute | solution.py:279
  106.2 0.8 copy.46
  107.0 0.8 copy.47
  (51 shorter events, 1.0 us)
Async XLA Ops:
  0.6 84.5 %copy-start = (bf16[5120,256]{1,0:T(8,128)(2,1)S(1)}, bf16[5120,256]{1,0:T(8,128)(2,1)}, u32[]{:S(2)}) copy-start(bf16[5120,256]{1,0:T(8,128)(2,1)} %param.15) | copy-start | bytes 7864324
  0.7 5.8 %copy-start.2 = (bf16[128,2,16,128]{3,2,1,0:T(8,128)(2,1)S(1)}, bf16[128,2,16,128]{3,2,1,0:T(8,128)(2,1)}, u32[]{:S(2)}) copy-start(bf16[128,2,16,128]{3,2,1,0:T(8,128)(2,1)} %param.9) | copy-start | bytes 3145732
  0.7 6.0 %copy-start.3 = (bf16[128,2,16,128]{3,2,1,0:T(8,128)(2,1)S(1)}, bf16[128,2,16,128]{3,2,1,0:T(8,128)(2,1)}, u32[]{:S(2)}) copy-start(bf16[128,2,16,128]{3,2,1,0:T(8,128)(2,1)} %param.12) | copy-start | bytes 3145732
  2.8 10.3 %collective-permute-start.2 = (bf16[640,128]{1,0:T(8,128)(2,1)S(1)}, bf16[640,128]{1,0:T(8,128)(2,1)S(1)}, u32[]{:S(2)}, u32[]{:S(2)}) collective-permute-start(bf16[640,128]{1,0:T(8,128)(2,1)S(1)} %pad_maximum_fusion.4), channel_id=1, source_target_pairs={{0,16},{16,0},{32,48},{48,32},{64,80},{80,64},{96,112},{112,96},{1... | collective-permute-start | bytes 491528 | tf_op jit(solution)/shard_map/ppermute | solution.py:279
  8.3 10.7 %copy-start.6 = (s32[16]{0:T(128)S(1)}, s32[16]{0:T(128)}, u32[]{:S(2)}) copy-start(s32[16]{0:T(128)} %param.17) | copy-start | bytes 196
  9.2 22.7 %collective-permute-start = (bf16[2,1024,128]{2,1,0:T(8,128)(2,1)}, bf16[2,1024,128]{2,1,0:T(8,128)(2,1)}, u32[]{:S(2)}, u32[]{:S(2)}) collective-permute-start(bf16[2,1024,128]{2,1,0:T(8,128)(2,1)} %bitcast.13), channel_id=1, source_target_pairs={{0,16},{16,0},{32,48},{48,32},{64,80},{80,64},{96,112},{112,96},{1... | collective-permute-start | bytes 1572872 | tf_op jit(solution)/shard_map/ppermute | solution.py:279
  10.1 24.6 %collective-permute-start.1 = (bf16[2,1024,128]{2,1,0:T(8,128)(2,1)}, bf16[2,1024,128]{2,1,0:T(8,128)(2,1)}, u32[]{:S(2)}, u32[]{:S(2)}) collective-permute-start(bf16[2,1024,128]{2,1,0:T(8,128)(2,1)} %bitcast.19), channel_id=1, source_target_pairs={{0,16},{16,0},{32,48},{48,32},{64,80},{80,64},{96,112},{112,96},{1... | collective-permute-start | bytes 1572872 | tf_op jit(solution)/shard_map/ppermute | solution.py:279
  13.2 12.9 %collective-permute-start.3 = (bf16[1280,128]{1,0:T(8,128)(2,1)S(1)}, bf16[1280,128]{1,0:T(8,128)(2,1)S(1)}, u32[]{:S(2)}, u32[]{:S(2)}) collective-permute-start(bf16[1280,128]{1,0:T(8,128)(2,1)S(1)} %pad_maximum_fusion.2.refs_4_), channel_id=1, source_target_pairs={{0,32},{16,48},{32,64},{48,80},{64,96},{80,112},{96,0},{112,16},{1... | collective-permute-start | bytes 983048 | tf_op jit(solution)/shard_map/ppermute | solution.py:287
  15.0 16.6 %collective-permute-start.4 = (bf16[1280,128]{1,0:T(8,128)(2,1)S(1)}, bf16[1280,128]{1,0:T(8,128)(2,1)}, u32[]{:S(2)}, u32[]{:S(2)}) collective-permute-start(bf16[1280,128]{1,0:T(8,128)(2,1)S(1)} %pad_maximum_fusion.2.refs_4_), channel_id=1, source_target_pairs={{0,64},{16,80},{32,96},{48,112},{64,0},{80,16},{96,32},{112,48},{1... | collective-permute-start | bytes 983048 | tf_op jit(solution)/shard_map/ppermute | solution.py:287
  18.3 13.7 %collective-permute-start.5 = (bf16[1280,128]{1,0:T(8,128)(2,1)S(1)}, bf16[1280,128]{1,0:T(8,128)(2,1)}, u32[]{:S(2)}, u32[]{:S(2)}) collective-permute-start(bf16[1280,128]{1,0:T(8,128)(2,1)S(1)} %pad_maximum_fusion.2.refs_4_), channel_id=1, source_target_pairs={{0,96},{16,112},{32,0},{48,16},{64,32},{80,48},{96,64},{112,80},{1... | collective-permute-start | bytes 983048 | tf_op jit(solution)/shard_map/ppermute | solution.py:287
  49.9 13.8 %collective-permute-start.6 = (bf16[256,128]{1,0:T(8,128)(2,1)}, bf16[256,128]{1,0:T(8,128)(2,1)S(1)}, u32[]{:S(2)}, u32[]{:S(2)}) collective-permute-start(bf16[256,128]{1,0:T(8,128)(2,1)} %get-tuple-element.28), channel_id=1, source_target_pairs={{0,96},{16,112},{32,0},{48,16},{64,32},{80,48},{96,64},{112,80},{1... | collective-permute-start | bytes 196616 | tf_op jit(solution)/shard_map/ppermute | solution.py:287
  57.0 6.9 %collective-permute-start.7 = (bf16[256,128]{1,0:T(8,128)(2,1)}, bf16[256,128]{1,0:T(8,128)(2,1)S(1)}, u32[]{:S(2)}, u32[]{:S(2)}) collective-permute-start(bf16[256,128]{1,0:T(8,128)(2,1)} %get-tuple-element.29), channel_id=1, source_target_pairs={{0,64},{16,80},{32,96},{48,112},{64,0},{80,16},{96,32},{112,48},{1... | collective-permute-start | bytes 196616 | tf_op jit(solution)/shard_map/ppermute | solution.py:287
  62.0 4.6 %collective-permute-start.8 = (bf16[256,128]{1,0:T(8,128)(2,1)}, bf16[256,128]{1,0:T(8,128)(2,1)S(1)}, u32[]{:S(2)}, u32[]{:S(2)}) collective-permute-start(bf16[256,128]{1,0:T(8,128)(2,1)} %get-tuple-element.30), channel_id=1, source_target_pairs={{0,32},{16,48},{32,64},{48,80},{64,96},{80,112},{96,0},{112,16},{1... | collective-permute-start | bytes 196616 | tf_op jit(solution)/shard_map/ppermute | solution.py:287
  62.8 17.5 %collective-permute-start.13 = (bf16[2,1024,128]{2,1,0:T(8,128)(2,1)}, bf16[2,1024,128]{2,1,0:T(8,128)(2,1)S(1)}, u32[]{:S(2)}, u32[]{:S(2)}) collective-permute-start(bf16[2,1024,128]{2,1,0:T(8,128)(2,1)} %get-tuple-element.33), channel_id=1, source_target_pairs={{0,16},{16,0},{32,48},{48,32},{64,80},{80,64},{96,112},{112,96},{1... | collective-permute-start | bytes 1572872 | tf_op jit(solution)/shard_map/ppermute | solution.py:279
  67.5 4.3 %collective-permute-start.9 = (f32[256,128]{1,0:T(8,128)S(1)}, f32[256,128]{1,0:T(8,128)S(1)}, u32[]{:S(2)}, u32[]{:S(2)}) collective-permute-start(f32[256,128]{1,0:T(8,128)S(1)} %convert_add_fusion), channel_id=1, source_target_pairs={{0,2},{2,0},{4,6},{6,4},{8,10},{10,8},{12,14},{14,12},{1,3},{3,1},... | collective-permute-start | bytes 393224 | tf_op jit(solution)/shard_map/ppermute | solution.py:334
  71.8 4.0 %collective-permute-start.10 = (bf16[256,128]{1,0:T(8,128)(2,1)S(1)}, bf16[256,128]{1,0:T(8,128)(2,1)S(1)}, u32[]{:S(2)}, u32[]{:S(2)}) collective-permute-start(bf16[256,128]{1,0:T(8,128)(2,1)S(1)} %add_convert_fusion.3), channel_id=1, source_target_pairs={{0,4},{2,6},{4,0},{6,2},{8,12},{10,14},{12,8},{14,10},{1,5},{3,7},... | collective-permute-start | bytes 196616 | tf_op jit(solution)/shard_map/ppermute | solution.py:334
  73.2 5.6 %collective-permute-start.11 = (bf16[256,128]{1,0:T(8,128)(2,1)S(1)}, bf16[256,128]{1,0:T(8,128)(2,1)S(1)}, u32[]{:S(2)}, u32[]{:S(2)}) collective-permute-start(bf16[256,128]{1,0:T(8,128)(2,1)S(1)} %add_convert_fusion.3), channel_id=1, source_target_pairs={{0,8},{2,10},{4,12},{6,14},{8,0},{10,2},{12,4},{14,6},{1,9},{3,11}... | collective-permute-start | bytes 196616 | tf_op jit(solution)/shard_map/ppermute | solution.py:334
  75.8 4.5 %collective-permute-start.12 = (bf16[256,128]{1,0:T(8,128)(2,1)S(1)}, bf16[256,128]{1,0:T(8,128)(2,1)S(1)}, u32[]{:S(2)}, u32[]{:S(2)}) collective-permute-start(bf16[256,128]{1,0:T(8,128)(2,1)S(1)} %add_convert_fusion.3), channel_id=1, source_target_pairs={{0,12},{2,14},{4,8},{6,10},{8,4},{10,6},{12,0},{14,2},{1,13},{3,15... | collective-permute-start | bytes 196616 | tf_op jit(solution)/shard_map/ppermute | solution.py:334
  80.3 4.8 %collective-permute-start.14 = (bf16[2,64,128]{2,1,0:T(8,128)(2,1)S(1)}, bf16[2,64,128]{2,1,0:T(8,128)(2,1)S(1)}, u32[]{:S(2)}, u32[]{:S(2)}) collective-permute-start(bf16[2,64,128]{2,1,0:T(8,128)(2,1)S(1)} %slice_bitcast_fusion.8), channel_id=1, source_target_pairs={{0,16},{16,0},{32,48},{48,32},{64,80},{80,64},{96,112},{112,96},{1... | collective-permute-start | bytes 98312 | tf_op jit(solution)/shard_map/ppermute | solution.py:279
  81.0 5.1 %copy-start.1 = (bf16[5120,256]{1,0:T(8,128)(2,1)S(1)}, bf16[5120,256]{1,0:T(8,128)(2,1)}, u32[]{:S(2)}) copy-start(bf16[5120,256]{1,0:T(8,128)(2,1)} %param.16) | copy-start | bytes 7864324
  81.0 9.0 %collective-permute-start.15 = (bf16[2,512,128]{2,1,0:T(8,128)(2,1)}, bf16[2,512,128]{2,1,0:T(8,128)(2,1)S(1)}, u32[]{:S(2)}, u32[]{:S(2)}) collective-permute-start(bf16[2,512,128]{2,1,0:T(8,128)(2,1)} %get-tuple-element.44), channel_id=1, source_target_pairs={{32,0},{48,16},{64,32},{80,48},{96,64},{112,80},{33,1},{49,17},{65... | collective-permute-start | bytes 786440 | tf_op jit(solution)/shard_map/ppermute | solution.py:287
  82.5 9.2 %collective-permute-start.16 = (bf16[2,512,128]{2,1,0:T(8,128)(2,1)}, bf16[2,512,128]{2,1,0:T(8,128)(2,1)S(1)}, u32[]{:S(2)}, u32[]{:S(2)}) collective-permute-start(bf16[2,512,128]{2,1,0:T(8,128)(2,1)} %get-tuple-element.45), channel_id=1, source_target_pairs={{64,0},{80,16},{96,32},{112,48},{65,1},{81,17},{97,33},{113,49},{6... | collective-permute-start | bytes 786440 | tf_op jit(solution)/shard_map/ppermute | solution.py:287
  83.8 16.1 %collective-permute-start.17 = (bf16[2,512,128]{2,1,0:T(8,128)(2,1)}, bf16[2,512,128]{2,1,0:T(8,128)(2,1)S(1)}, u32[]{:S(2)}, u32[]{:S(2)}) collective-permute-start(bf16[2,512,128]{2,1,0:T(8,128)(2,1)} %get-tuple-element.46), channel_id=1, source_target_pairs={{96,0},{112,16},{97,1},{113,17},{98,2},{114,18},{99,3},{115,19},{1... | collective-permute-start | bytes 786440 | tf_op jit(solution)/shard_map/ppermute | solution.py:287
  86.1 1.9 %copy-start.4 = (bf16[2,1024,128]{2,1,0:T(8,128)(2,1)S(1)}, bf16[2,1024,128]{2,1,0:T(8,128)(2,1)}, u32[]{:S(2)}) copy-start(bf16[2,1024,128]{2,1,0:T(8,128)(2,1)} %get-tuple-element.26) | copy-start | bytes 1572868
  87.1 15.5 %collective-permute-start.19 = (bf16[64,2560]{1,0:T(8,128)(2,1)S(1)}, bf16[64,2560]{1,0:T(8,128)(2,1)S(1)}, u32[]{:S(2)}, u32[]{:S(2)}) collective-permute-start(bf16[64,2560]{1,0:T(8,128)(2,1)S(1)} %dynamic-slice_convert_fusion), channel_id=1, source_target_pairs={{0,1},{1,0},{2,3},{3,2},{4,5},{5,4},{6,7},{7,6},{8,9},{9,8},{10,11... | collective-permute-start | bytes 983048 | tf_op jit(solution)/shard_map/ppermute | solution.py:367
  88.1 11.8 %copy-start.5 = (bf16[2,512,128]{2,1,0:T(8,128)(2,1)S(1)}, bf16[2,512,128]{2,1,0:T(8,128)(2,1)}, u32[]{:S(2)}) copy-start(bf16[2,512,128]{2,1,0:T(8,128)(2,1)} %get-tuple-element.43) | copy-start | bytes 786436
  100.1 6.1 %collective-permute-start.18 = (bf16[2,2,128,128]{3,2,1,0:T(8,128)(2,1)S(1)}, bf16[2,2,128,128]{3,2,1,0:T(8,128)(2,1)S(1)}, u32[]{:S(2)}, u32[]{:S(2)}) collective-permute-start(bf16[2,2,128,128]{3,2,1,0:T(8,128)(2,1)S(1)} %slice_bitcast_fusion.6), channel_id=1, source_target_pairs={{0,16},{16,0},{32,48},{48,32},{64,80},{80,64},{96,112},{112,96},{1... | collective-permute-start | bytes 393224 | tf_op jit(solution)/shard_map/ppermute | solution.py:279

commit v2 on v1

--- a/solution.py
+++ b/solution.py
@@ -339,20 +339,22 @@
     dq_got = swap(dq_away)
     share = (share + exchange(share, 1)).astype(BF16)
     terms = [share] + [exchange(share, step) for step in range(2, group_size, 2)]
-    terms[1], dkv[1] = lax.optimization_barrier((terms[1], dkv[1]))
-    near = shift(dkv[1], -1, False)
+    middle = zs // 2
+    terms[1], dkv[middle] = lax.optimization_barrier((terms[1], dkv[middle]))
+    early = shift(dkv.pop(middle), -middle, False)
     *terms, dq_got = lax.optimization_barrier((*terms, dq_got))
     terms = [x.astype(F32) for x in terms]
     while len(terms) > 1:
         terms = [terms[i] + terms[i + 1] for i in range(0, len(terms), 2)]
-    share, *dkv[2:] = lax.optimization_barrier((terms[0].astype(BF16), *dkv[2:]))
+    share, *dkv[1:] = lax.optimization_barrier((terms[0].astype(BF16), *dkv[1:]))
     low = share.reshape(2, 2, prows, width)
-    low = jnp.concatenate(in_order(low[:, 0], swap(low[:, 1])), 2)
+    low_got, early = lax.optimization_barrier((swap(low[:, 1]), early))
+    low = jnp.concatenate(in_order(low[:, 0], low_got), 2)
     projected = dot_nt(low[0], key_matrix) + dot_nt(low[1], value_matrix)
 
-    total = dkv[0].astype(F32) + near.astype(F32)
-    for s in range(2, zs):
-        total = total + shift(dkv[s], -s, False).astype(F32)
+    total = dkv[0].astype(F32) + early.astype(F32)
+    for s, part in zip([s for s in range(1, zs) if s != middle], dkv[1:]):
+        total = total + shift(part, -s, False).astype(F32)
     total = total.reshape(resp_count, 2, 2, tokens, width).astype(BF16)
     grads = in_order(total[:, :, 0], swap(total[:, :, 1]))
     grads = jnp.stack(grads, 2).transpose(1, 3, 0, 2, 4)

time: 108 us -> 102 us (0.944); the launches traced: 108 us -> 101 us
  waiting for transfers between devices: 29.7 us -> 25.2 us
  starting transfers between devices: 41.7 us -> 39.1 us
    ppermute x9, starting transfers between devices: 22.8 us -> 17.8 us  [shift(): return lax.ppermute(x, 'prefix', pairs)]
    ppermute x4, starting transfers between devices: 7.27 us -> 11.7 us  [exchange(): return lax.ppermute(x, 'group', [(i, i ^ step) for i in range(group_size)])]
    ppermute x9, waiting for transfers between devices: 18.7 us -> 14.7 us  [shift(): return lax.ppermute(x, 'prefix', pairs)]
    ppermute x4, waiting for transfers between devices: 5.44 us -> 2.63 us  [exchange(): return lax.ppermute(x, 'group', [(i, i ^ step) for i in range(group_size)])]
    ppermute x6, starting transfers between devices: 10.6 us -> 9.16 us  [swap(): return lax.ppermute(x, 'prefix', [(i, i ^ 1) for i in range(prefix_size)])]
    ppermute x1, waiting for transfers between devices: 0.01 us -> 1.44 us  [per_device(): got = lax.ppermute(away, 'tensor', [(0, 1), (1, 0)])]
  transfers between devices with their start and end apart: 20 -> 20, of which waited for: 11 -> 11; matrix products, arithmetic and copies ran while one was open for 13% -> 14% of each run, Pallas kernels for 0% -> 0%
where the time goes in v2:
time: 102 us; the launch traced here: 101 us
  starting transfers between devices  39.1 us (38%)
  waiting for transfers between devices  25.2 us (25%)
  Pallas kernels  15.1 us (15%)
  local copies, waits for them, and re-layouts  11.2 us (11%)
  other arithmetic  4.75 us (5%)
  between operations  3.54 us (3%)
  matrix products  1.83 us (2%)
    ppermute x9, starting transfers between devices, shift(): return lax.ppermute(x, 'prefix', pairs)  17.8 us
    pallas_call x1, Pallas kernels, attention(): pl.pallas_call(functools.partial(attention_kernel, tokens, prows, zs, cou...  15.1 us
    ppermute x9, waiting for transfers between devices, shift(): return lax.ppermute(x, 'prefix', pairs)  14.7 us
    ppermute x4, starting transfers between devices, exchange(): return lax.ppermute(x, 'group', [(i, i ^ step) for i in range(group_size)])  11.7 us
    ppermute x6, starting transfers between devices, swap(): return lax.ppermute(x, 'prefix', [(i, i ^ 1) for i in range(prefix_size)])  9.16 us
    ppermute x6, waiting for transfers between devices, swap(): return lax.ppermute(x, 'prefix', [(i, i ^ 1) for i in range(prefix_size)])  6.43 us
    transpose x2, local copies, waits for them, and re-layouts, per_device(): own = own.transpose(0, 2, 1, 3).reshape(2, factor * tokens, width)  3.88 us
    ppermute x4, waiting for transfers between devices, exchange(): return lax.ppermute(x, 'group', [(i, i ^ step) for i in range(group_size)])  2.63 us
  transfers between devices with their start and end apart: 20, of which 11 were waited for; matrix products, arithmetic and copies ran while one was open for 14% of the time, Pallas kernels for 0%

profile of v2, /device:TPU:1, one launch (start us, length us, event | category | flops | bytes accessed | tf_op | source)
XLA Modules:
  0.0 100.7 jit_solution(7914622578688381868)
XLA Ops:
  0.7 1.2 %copy_bitcast_fusion = (bf16[1,128,2,2,128]{4,1,0,2,3:T(8,128)(2,1)S(1)}, bf16[1,128,2,2,128]{4,1,0,2,3:T(8,128)(2,1)S(1)}) fusion(bf16[128,2,2,128]{3,2,1,0:T(2,128)(2,1)} %param.11, bf16[128,2,2,128]{3,2,1,0:T(2,128)(2,1)} %param.10), kind=kLoop, calls=%fused_computation.32 | loop fusion | bytes 524288 | tf_op jit(solution)/shard_map/stack | solution.py:295
  1.9 0.9 copy_bitcast_fusion.2
  2.8 3.7 %collective-permute-start.2 = (bf16[640,128]{1,0:T(8,128)(2,1)S(1)}, bf16[640,128]{1,0:T(8,128)(2,1)S(1)}, u32[]{:S(2)}, u32[]{:S(2)}) collective-permute-start(bf16[640,128]{1,0:T(8,128)(2,1)S(1)} %pad_maximum_fusion.4), channel_id=1, source_target_pairs={{0,16},{16,0},{32,48},{48,32},{64,80},{80,64},{96,112},{112,96},{1... | collective-permute-start | bytes 491528 | tf_op jit(solution)/shard_map/ppermute | solution.py:279
  6.5 0.2 slice_bitcast_fusion.1
  6.7 0.2 slice_bitcast_fusion
  6.9 1.5 %select_bitcast_fusion = (bf16[2,8,128,128]{3,1,2,0:T(8,128)(2,1)S(1)}, bf16[2,8,128,128]{3,1,2,0:T(8,128)(2,1)}, bf16[2,8,128,128]{3,1,2,0:T(8,128)(2,1)}, bf16[2,8,128,128]{3,1,2,0:T(8,128)(2,1)S(1)}) fusion(pred[]{:T(512)S(6)} %eq.5, bf16[1,128,16,128]{3,2,1,0:T(8,128)(2,1)S(1)} %get-tuple-element.62, bf16[1,128,16,128]{3,2,1,0:T(8,128)(2,1)S(1)} %get-tuple-element.60, ...), kind=kLoop, calls=%fused_computation.13 | loop fusion | flops 7340032 | bytes 4194305 | tf_op jit(solution)/shard_map/transpose | solution.py:319
  8.3 0.9 copy.31
  9.3 0.9 copy.34
  10.1 2.9 %collective-permute-start.1 = (bf16[2,1024,128]{2,1,0:T(8,128)(2,1)}, bf16[2,1024,128]{2,1,0:T(8,128)(2,1)}, u32[]{:S(2)}, u32[]{:S(2)}) collective-permute-start(bf16[2,1024,128]{2,1,0:T(8,128)(2,1)} %bitcast.19), channel_id=1, source_target_pairs={{0,16},{16,0},{32,48},{48,32},{64,80},{80,64},{96,112},{112,96},{1... | collective-permute-start | bytes 1572872 | tf_op jit(solution)/shard_map/ppermute | solution.py:279
  13.2 1.7 %collective-permute-start.3 = (bf16[1280,128]{1,0:T(8,128)(2,1)S(1)}, bf16[1280,128]{1,0:T(8,128)(2,1)S(1)}, u32[]{:S(2)}, u32[]{:S(2)}) collective-permute-start(bf16[1280,128]{1,0:T(8,128)(2,1)S(1)} %pad_maximum_fusion.2.refs_4_), channel_id=1, source_target_pairs={{0,32},{16,48},{32,64},{48,80},{64,96},{80,112},{96,0},{112,16},{1... | collective-permute-start | bytes 983048 | tf_op jit(solution)/shard_map/ppermute | solution.py:287
  15.0 3.3 %collective-permute-start.4 = (bf16[1280,128]{1,0:T(8,128)(2,1)S(1)}, bf16[1280,128]{1,0:T(8,128)(2,1)}, u32[]{:S(2)}, u32[]{:S(2)}) collective-permute-start(bf16[1280,128]{1,0:T(8,128)(2,1)S(1)} %pad_maximum_fusion.2.refs_4_), channel_id=1, source_target_pairs={{0,64},{16,80},{32,96},{48,112},{64,0},{80,16},{96,32},{112,48},{1... | collective-permute-start | bytes 983048 | tf_op jit(solution)/shard_map/ppermute | solution.py:287
  18.3 0.7 collective-permute-start.5
  19.1 0.6 fusion.11
  22.2 1.9 %copy.30 = bf16[2,8,128,128]{3,2,1,0:T(8,128)(2,1)} copy(bf16[2,8,128,128]{3,1,2,0:T(8,128)(2,1)} %get-tuple-element.78) | data formatting | bytes 1048576 | tf_op jit(solution)/shard_map/transpose | solution.py:318
  24.1 1.9 %copy.33 = bf16[2,8,128,128]{3,2,1,0:T(8,128)(2,1)} copy(bf16[2,8,128,128]{3,1,2,0:T(8,128)(2,1)} %get-tuple-element.59) | data formatting | bytes 1048576 | tf_op jit(solution)/shard_map/transpose | solution.py:318
  26.2 5.4 %collective-permute-done.4.refs_6_ = bf16[1280,128]{1,0:T(8,128)(2,1)} collective-permute-done((bf16[1280,128]{1,0:T(8,128)(2,1)S(1)}, bf16[1280,128]{1,0:T(8,128)(2,1)}, u32[]{:S(2)}, u32[]{:S(2)}) %collective-permute-start.4) | collective-permute-done | bytes 327712 | tf_op jit(solution)/shard_map/ppermute | solution.py:287
  31.6 0.3 collective-permute-done.5.refs_7_
  31.9 2.8 %collective-permute-done.1.refs_3_ = bf16[2,1024,128]{2,1,0:T(8,128)(2,1)} collective-permute-done((bf16[2,1024,128]{2,1,0:T(8,128)(2,1)}, bf16[2,1024,128]{2,1,0:T(8,128)(2,1)}, u32[]{:S(2)}, u32[]{:S(2)}) %collective-permute-start.1) | collective-permute-done | bytes 524320 | tf_op jit(solution)/shard_map/ppermute | solution.py:279
  34.8 15.1 %attention_grad.1 = (bf16[2,1024,128]{2,1,0:T(8,128)(2,1)}, bf16[2,1024,128]{2,1,0:T(8,128)(2,1)}, bf16[2,512,128]{2,1,0:T(8,128)(2,1)}, bf16[2,512,128]{2,1,0:T...) custom-call(s32[6]{0:T(128)S(1)} %stack.68.meta, ...), custom_call_target="tpu_custom_call" | custom-call | flops 8053063680 | bytes 8388608 | tf_op jit(solution)/shard_map/attention_grad/pallas_call | solution.py:240
  49.9 7.7 %collective-permute-start.7 = (bf16[256,128]{1,0:T(8,128)(2,1)}, bf16[256,128]{1,0:T(8,128)(2,1)S(1)}, u32[]{:S(2)}, u32[]{:S(2)}) collective-permute-start(bf16[256,128]{1,0:T(8,128)(2,1)} %get-tuple-element.31), channel_id=1, source_target_pairs={{0,64},{16,80},{32,96},{48,112},{64,0},{80,16},{96,32},{112,48},{1... | collective-permute-start | bytes 196616 | tf_op jit(solution)/shard_map/ppermute | solution.py:287
  57.6 0.2 collective-permute-start.8
  57.8 1.0 %collective-permute-start.13 = (bf16[2,1024,128]{2,1,0:T(8,128)(2,1)}, bf16[2,1024,128]{2,1,0:T(8,128)(2,1)S(1)}, u32[]{:S(2)}, u32[]{:S(2)}) collective-permute-start(bf16[2,1024,128]{2,1,0:T(8,128)(2,1)} %get-tuple-element.35), channel_id=1, source_target_pairs={{0,16},{16,0},{32,48},{48,32},{64,80},{80,64},{96,112},{112,96},{1... | collective-permute-start | bytes 1572872 | tf_op jit(solution)/shard_map/ppermute | solution.py:279
  58.8 0.6 collective-permute-done.7
  59.5 2.7 %collective-permute-done.8 = bf16[256,128]{1,0:T(8,128)(2,1)S(1)} collective-permute-done((bf16[256,128]{1,0:T(8,128)(2,1)}, bf16[256,128]{1,0:T(8,128)(2,1)S(1)}, u32[]{:S(2)}, u32[]{:S(2)}) %collective-permute-start.8) | collective-permute-done | bytes 65568 | tf_op jit(solution)/shard_map/ppermute | solution.py:287
  62.1 0.9 convert_add_fusion
  63.0 7.8 %collective-permute-start.9 = (f32[256,128]{1,0:T(8,128)S(1)}, f32[256,128]{1,0:T(8,128)S(1)}, u32[]{:S(2)}, u32[]{:S(2)}) collective-permute-start(f32[256,128]{1,0:T(8,128)S(1)} %convert_add_fusion), channel_id=1, source_target_pairs={{0,2},{2,0},{4,6},{6,4},{8,10},{10,8},{12,14},{14,12},{1,3},{3,1},... | collective-permute-start | bytes 393224 | tf_op jit(solution)/shard_map/ppermute | solution.py:334
  70.8 1.0 collective-permute-done.9
  71.9 1.0 collective-permute-start.11
  72.9 2.9 %collective-permute-start.12 = (bf16[256,128]{1,0:T(8,128)(2,1)S(1)}, bf16[256,128]{1,0:T(8,128)(2,1)S(1)}, u32[]{:S(2)}, u32[]{:S(2)}) collective-permute-start(bf16[256,128]{1,0:T(8,128)(2,1)S(1)} %add_convert_fusion.3), channel_id=1, source_target_pairs={{0,12},{2,14},{4,8},{6,10},{8,4},{10,6},{12,0},{14,2},{1,13},{3,15... | collective-permute-start | bytes 196616 | tf_op jit(solution)/shard_map/ppermute | solution.py:334
  75.8 1.3 %collective-permute-start.15 = (bf16[2,512,128]{2,1,0:T(8,128)(2,1)}, bf16[2,512,128]{2,1,0:T(8,128)(2,1)S(1)}, u32[]{:S(2)}, u32[]{:S(2)}) collective-permute-start(bf16[2,512,128]{2,1,0:T(8,128)(2,1)} %get-tuple-element.43), channel_id=1, source_target_pairs={{64,0},{80,16},{96,32},{112,48},{65,1},{81,17},{97,33},{113,49},{6... | collective-permute-start | bytes 786440 | tf_op jit(solution)/shard_map/ppermute | solution.py:287
  77.1 1.6 %collective-permute-done.12 = bf16[256,128]{1,0:T(8,128)(2,1)S(1)} collective-permute-done((bf16[256,128]{1,0:T(8,128)(2,1)S(1)}, bf16[256,128]{1,0:T(8,128)(2,1)S(1)}, u32[]{:S(2)}, u32[]{:S(2)}) %collective-permute-start.12) | collective-permute-done | bytes 65568 | tf_op jit(solution)/shard_map/ppermute | solution.py:334
  78.8 0.5 collective-permute-start.14
  79.2 1.5 %collective-permute-start.16 = (bf16[2,512,128]{2,1,0:T(8,128)(2,1)}, bf16[2,512,128]{2,1,0:T(8,128)(2,1)S(1)}, u32[]{:S(2)}, u32[]{:S(2)}) collective-permute-start(bf16[2,512,128]{2,1,0:T(8,128)(2,1)} %get-tuple-element.49), channel_id=1, source_target_pairs={{32,0},{48,16},{64,32},{80,48},{96,64},{112,80},{33,1},{49,17},{65... | collective-permute-start | bytes 786440 | tf_op jit(solution)/shard_map/ppermute | solution.py:287
  80.8 1.3 %collective-permute-start.17 = (bf16[2,512,128]{2,1,0:T(8,128)(2,1)}, bf16[2,512,128]{2,1,0:T(8,128)(2,1)S(1)}, u32[]{:S(2)}, u32[]{:S(2)}) collective-permute-start(bf16[2,512,128]{2,1,0:T(8,128)(2,1)} %get-tuple-element.50), channel_id=1, source_target_pairs={{96,0},{112,16},{97,1},{113,17},{98,2},{114,18},{99,3},{115,19},{1... | collective-permute-start | bytes 786440 | tf_op jit(solution)/shard_map/ppermute | solution.py:287
  82.1 3.7 %collective-permute-done.15 = bf16[2,512,128]{2,1,0:T(8,128)(2,1)S(1)} collective-permute-done((bf16[2,512,128]{2,1,0:T(8,128)(2,1)}, bf16[2,512,128]{2,1,0:T(8,128)(2,1)S(1)}, u32[]{:S(2)}, u32[]{:S(2)}) %collective-permute-start.15) | collective-permute-done | bytes 262176 | tf_op jit(solution)/shard_map/ppermute | solution.py:287
  85.9 0.9 fusion.4
  86.8 0.9 convolution_add_fusion
  87.8 0.4 collective-permute-start.19
  88.2 0.3 copy.42
  88.6 0.3 copy.43
  88.9 1.2 %maximum_bitcast_fusion = bf16[128,2,16,128]{3,2,1,0:T(8,128)(2,1)} fusion(bf16[2,8,128,128]{3,1,0,2:T(8,128)(2,1)S(1)} %copy.43, bf16[2,8,128,128]{3,1,0,2:T(8,128)(2,1)S(1)} %copy.42), kind=kLoop, calls=%fused_computation.5 | loop fusion | flops 2097152 | bytes 2097152 | tf_op jit(solution)/shard_map/transpose | solution.py:368
  90.1 1.9 %collective-permute-done.17 = bf16[2,512,128]{2,1,0:T(8,128)(2,1)S(1)} collective-permute-done((bf16[2,512,128]{2,1,0:T(8,128)(2,1)}, bf16[2,512,128]{2,1,0:T(8,128)(2,1)S(1)}, u32[]{:S(2)}, u32[]{:S(2)}) %collective-permute-start.17) | collective-permute-done | bytes 262176 | tf_op jit(solution)/shard_map/ppermute | solution.py:287
  92.2 1.1 %collective-permute-start.18 = (bf16[2,2,128,128]{3,2,1,0:T(8,128)(2,1)S(1)}, bf16[2,2,128,128]{3,2,1,0:T(8,128)(2,1)S(1)}, u32[]{:S(2)}, u32[]{:S(2)}) collective-permute-start(bf16[2,2,128,128]{3,2,1,0:T(8,128)(2,1)S(1)} %slice_bitcast_fusion.6), channel_id=1, source_target_pairs={{0,16},{16,0},{32,48},{48,32},{64,80},{80,64},{96,112},{112,96},{1... | collective-permute-start | bytes 393224 | tf_op jit(solution)/shard_map/ppermute | solution.py:279
  93.2 1.4 %collective-permute-done.19 = bf16[64,2560]{1,0:T(8,128)(2,1)S(1)} collective-permute-done((bf16[64,2560]{1,0:T(8,128)(2,1)S(1)}, bf16[64,2560]{1,0:T(8,128)(2,1)S(1)}, u32[]{:S(2)}, u32[]{:S(2)}) %collective-permute-start.19) | collective-permute-done | bytes 327712 | tf_op jit(solution)/shard_map/ppermute | solution.py:369
  94.7 0.8 add_convert_fusion
  95.5 3.6 %collective-permute-done.18 = bf16[2,2,128,128]{3,2,1,0:T(8,128)(2,1)S(1)} collective-permute-done((bf16[2,2,128,128]{3,2,1,0:T(8,128)(2,1)S(1)}, bf16[2,2,128,128]{3,2,1,0:T(8,128)(2,1)S(1)}, u32[]{:S(2)}, u32[]{:S(2)}) %collective-permute-start.18) | collective-permute-done | bytes 131104 | tf_op jit(solution)/shard_map/ppermute | solution.py:279
  99.1 0.8 copy.46
  99.9 0.8 copy.47
  (51 shorter events, 1.0 us)
Async XLA Ops:
  0.6 85.2 %copy-start = (bf16[5120,256]{1,0:T(8,128)(2,1)S(1)}, bf16[5120,256]{1,0:T(8,128)(2,1)}, u32[]{:S(2)}) copy-start(bf16[5120,256]{1,0:T(8,128)(2,1)} %param.15) | copy-start | bytes 7864324
  0.7 5.8 %copy-start.2 = (bf16[128,2,16,128]{3,2,1,0:T(8,128)(2,1)S(1)}, bf16[128,2,16,128]{3,2,1,0:T(8,128)(2,1)}, u32[]{:S(2)}) copy-start(bf16[128,2,16,128]{3,2,1,0:T(8,128)(2,1)} %param.9) | copy-start | bytes 3145732
  0.7 6.0 %copy-start.3 = (bf16[128,2,16,128]{3,2,1,0:T(8,128)(2,1)S(1)}, bf16[128,2,16,128]{3,2,1,0:T(8,128)(2,1)}, u32[]{:S(2)}) copy-start(bf16[128,2,16,128]{3,2,1,0:T(8,128)(2,1)} %param.12) | copy-start | bytes 3145732
  2.8 10.3 %collective-permute-start.2 = (bf16[640,128]{1,0:T(8,128)(2,1)S(1)}, bf16[640,128]{1,0:T(8,128)(2,1)S(1)}, u32[]{:S(2)}, u32[]{:S(2)}) collective-permute-start(bf16[640,128]{1,0:T(8,128)(2,1)S(1)} %pad_maximum_fusion.4), channel_id=1, source_target_pairs={{0,16},{16,0},{32,48},{48,32},{64,80},{80,64},{96,112},{112,96},{1... | collective-permute-start | bytes 491528 | tf_op jit(solution)/shard_map/ppermute | solution.py:279
  8.3 10.7 %copy-start.6 = (s32[16]{0:T(128)S(1)}, s32[16]{0:T(128)}, u32[]{:S(2)}) copy-start(s32[16]{0:T(128)} %param.17) | copy-start | bytes 196
  9.2 22.7 %collective-permute-start = (bf16[2,1024,128]{2,1,0:T(8,128)(2,1)}, bf16[2,1024,128]{2,1,0:T(8,128)(2,1)}, u32[]{:S(2)}, u32[]{:S(2)}) collective-permute-start(bf16[2,1024,128]{2,1,0:T(8,128)(2,1)} %bitcast.13), channel_id=1, source_target_pairs={{0,16},{16,0},{32,48},{48,32},{64,80},{80,64},{96,112},{112,96},{1... | collective-permute-start | bytes 1572872 | tf_op jit(solution)/shard_map/ppermute | solution.py:279
  10.1 24.6 %collective-permute-start.1 = (bf16[2,1024,128]{2,1,0:T(8,128)(2,1)}, bf16[2,1024,128]{2,1,0:T(8,128)(2,1)}, u32[]{:S(2)}, u32[]{:S(2)}) collective-permute-start(bf16[2,1024,128]{2,1,0:T(8,128)(2,1)} %bitcast.19), channel_id=1, source_target_pairs={{0,16},{16,0},{32,48},{48,32},{64,80},{80,64},{96,112},{112,96},{1... | collective-permute-start | bytes 1572872 | tf_op jit(solution)/shard_map/ppermute | solution.py:279
  13.2 12.9 %collective-permute-start.3 = (bf16[1280,128]{1,0:T(8,128)(2,1)S(1)}, bf16[1280,128]{1,0:T(8,128)(2,1)S(1)}, u32[]{:S(2)}, u32[]{:S(2)}) collective-permute-start(bf16[1280,128]{1,0:T(8,128)(2,1)S(1)} %pad_maximum_fusion.2.refs_4_), channel_id=1, source_target_pairs={{0,32},{16,48},{32,64},{48,80},{64,96},{80,112},{96,0},{112,16},{1... | collective-permute-start | bytes 983048 | tf_op jit(solution)/shard_map/ppermute | solution.py:287
  15.0 16.6 %collective-permute-start.4 = (bf16[1280,128]{1,0:T(8,128)(2,1)S(1)}, bf16[1280,128]{1,0:T(8,128)(2,1)}, u32[]{:S(2)}, u32[]{:S(2)}) collective-permute-start(bf16[1280,128]{1,0:T(8,128)(2,1)S(1)} %pad_maximum_fusion.2.refs_4_), channel_id=1, source_target_pairs={{0,64},{16,80},{32,96},{48,112},{64,0},{80,16},{96,32},{112,48},{1... | collective-permute-start | bytes 983048 | tf_op jit(solution)/shard_map/ppermute | solution.py:287
  18.3 13.7 %collective-permute-start.5 = (bf16[1280,128]{1,0:T(8,128)(2,1)S(1)}, bf16[1280,128]{1,0:T(8,128)(2,1)}, u32[]{:S(2)}, u32[]{:S(2)}) collective-permute-start(bf16[1280,128]{1,0:T(8,128)(2,1)S(1)} %pad_maximum_fusion.2.refs_4_), channel_id=1, source_target_pairs={{0,96},{16,112},{32,0},{48,16},{64,32},{80,48},{96,64},{112,80},{1... | collective-permute-start | bytes 983048 | tf_op jit(solution)/shard_map/ppermute | solution.py:287
  49.9 9.0 %collective-permute-start.6 = (bf16[256,128]{1,0:T(8,128)(2,1)}, bf16[256,128]{1,0:T(8,128)(2,1)S(1)}, u32[]{:S(2)}, u32[]{:S(2)}) collective-permute-start(bf16[256,128]{1,0:T(8,128)(2,1)} %get-tuple-element.30), channel_id=1, source_target_pairs={{0,96},{16,112},{32,0},{48,16},{64,32},{80,48},{96,64},{112,80},{1... | collective-permute-start | bytes 196616 | tf_op jit(solution)/shard_map/ppermute | solution.py:287
  49.9 9.5 %collective-permute-start.7 = (bf16[256,128]{1,0:T(8,128)(2,1)}, bf16[256,128]{1,0:T(8,128)(2,1)S(1)}, u32[]{:S(2)}, u32[]{:S(2)}) collective-permute-start(bf16[256,128]{1,0:T(8,128)(2,1)} %get-tuple-element.31), channel_id=1, source_target_pairs={{0,64},{16,80},{32,96},{48,112},{64,0},{80,16},{96,32},{112,48},{1... | collective-permute-start | bytes 196616 | tf_op jit(solution)/shard_map/ppermute | solution.py:287
  57.6 4.5 %collective-permute-start.8 = (bf16[256,128]{1,0:T(8,128)(2,1)}, bf16[256,128]{1,0:T(8,128)(2,1)S(1)}, u32[]{:S(2)}, u32[]{:S(2)}) collective-permute-start(bf16[256,128]{1,0:T(8,128)(2,1)} %get-tuple-element.32), channel_id=1, source_target_pairs={{0,32},{16,48},{32,64},{48,80},{64,96},{80,112},{96,0},{112,16},{1... | collective-permute-start | bytes 196616 | tf_op jit(solution)/shard_map/ppermute | solution.py:287
  57.8 20.9 %collective-permute-start.13 = (bf16[2,1024,128]{2,1,0:T(8,128)(2,1)}, bf16[2,1024,128]{2,1,0:T(8,128)(2,1)S(1)}, u32[]{:S(2)}, u32[]{:S(2)}) collective-permute-start(bf16[2,1024,128]{2,1,0:T(8,128)(2,1)} %get-tuple-element.35), channel_id=1, source_target_pairs={{0,16},{16,0},{32,48},{48,32},{64,80},{80,64},{96,112},{112,96},{1... | collective-permute-start | bytes 1572872 | tf_op jit(solution)/shard_map/ppermute | solution.py:279
  63.0 8.8 %collective-permute-start.9 = (f32[256,128]{1,0:T(8,128)S(1)}, f32[256,128]{1,0:T(8,128)S(1)}, u32[]{:S(2)}, u32[]{:S(2)}) collective-permute-start(f32[256,128]{1,0:T(8,128)S(1)} %convert_add_fusion), channel_id=1, source_target_pairs={{0,2},{2,0},{4,6},{6,4},{8,10},{10,8},{12,14},{14,12},{1,3},{3,1},... | collective-permute-start | bytes 393224 | tf_op jit(solution)/shard_map/ppermute | solution.py:334
  71.8 3.9 %collective-permute-start.10 = (bf16[256,128]{1,0:T(8,128)(2,1)S(1)}, bf16[256,128]{1,0:T(8,128)(2,1)S(1)}, u32[]{:S(2)}, u32[]{:S(2)}) collective-permute-start(bf16[256,128]{1,0:T(8,128)(2,1)S(1)} %add_convert_fusion.3), channel_id=1, source_target_pairs={{0,4},{2,6},{4,0},{6,2},{8,12},{10,14},{12,8},{14,10},{1,5},{3,7},... | collective-permute-start | bytes 196616 | tf_op jit(solution)/shard_map/ppermute | solution.py:334
  71.9 5.1 %collective-permute-start.11 = (bf16[256,128]{1,0:T(8,128)(2,1)S(1)}, bf16[256,128]{1,0:T(8,128)(2,1)S(1)}, u32[]{:S(2)}, u32[]{:S(2)}) collective-permute-start(bf16[256,128]{1,0:T(8,128)(2,1)S(1)} %add_convert_fusion.3), channel_id=1, source_target_pairs={{0,8},{2,10},{4,12},{6,14},{8,0},{10,2},{12,4},{14,6},{1,9},{3,11}... | collective-permute-start | bytes 196616 | tf_op jit(solution)/shard_map/ppermute | solution.py:334
  72.9 5.8 %collective-permute-start.12 = (bf16[256,128]{1,0:T(8,128)(2,1)S(1)}, bf16[256,128]{1,0:T(8,128)(2,1)S(1)}, u32[]{:S(2)}, u32[]{:S(2)}) collective-permute-start(bf16[256,128]{1,0:T(8,128)(2,1)S(1)} %add_convert_fusion.3), channel_id=1, source_target_pairs={{0,12},{2,14},{4,8},{6,10},{8,4},{10,6},{12,0},{14,2},{1,13},{3,15... | collective-permute-start | bytes 196616 | tf_op jit(solution)/shard_map/ppermute | solution.py:334
  75.8 10.0 %collective-permute-start.15 = (bf16[2,512,128]{2,1,0:T(8,128)(2,1)}, bf16[2,512,128]{2,1,0:T(8,128)(2,1)S(1)}, u32[]{:S(2)}, u32[]{:S(2)}) collective-permute-start(bf16[2,512,128]{2,1,0:T(8,128)(2,1)} %get-tuple-element.43), channel_id=1, source_target_pairs={{64,0},{80,16},{96,32},{112,48},{65,1},{81,17},{97,33},{113,49},{6... | collective-permute-start | bytes 786440 | tf_op jit(solution)/shard_map/ppermute | solution.py:287
  78.8 7.1 %collective-permute-start.14 = (bf16[2,64,128]{2,1,0:T(8,128)(2,1)S(1)}, bf16[2,64,128]{2,1,0:T(8,128)(2,1)S(1)}, u32[]{:S(2)}, u32[]{:S(2)}) collective-permute-start(bf16[2,64,128]{2,1,0:T(8,128)(2,1)S(1)} %slice_bitcast_fusion.8), channel_id=1, source_target_pairs={{0,16},{16,0},{32,48},{48,32},{64,80},{80,64},{96,112},{112,96},{1... | collective-permute-start | bytes 98312 | tf_op jit(solution)/shard_map/ppermute | solution.py:279
  79.2 7.5 %copy-start.1 = (bf16[5120,256]{1,0:T(8,128)(2,1)S(1)}, bf16[5120,256]{1,0:T(8,128)(2,1)}, u32[]{:S(2)}) copy-start(bf16[5120,256]{1,0:T(8,128)(2,1)} %param.16) | copy-start | bytes 7864324
  79.2 10.8 %collective-permute-start.16 = (bf16[2,512,128]{2,1,0:T(8,128)(2,1)}, bf16[2,512,128]{2,1,0:T(8,128)(2,1)S(1)}, u32[]{:S(2)}, u32[]{:S(2)}) collective-permute-start(bf16[2,512,128]{2,1,0:T(8,128)(2,1)} %get-tuple-element.49), channel_id=1, source_target_pairs={{32,0},{48,16},{64,32},{80,48},{96,64},{112,80},{33,1},{49,17},{65... | collective-permute-start | bytes 786440 | tf_op jit(solution)/shard_map/ppermute | solution.py:287
  80.8 11.2 %collective-permute-start.17 = (bf16[2,512,128]{2,1,0:T(8,128)(2,1)}, bf16[2,512,128]{2,1,0:T(8,128)(2,1)S(1)}, u32[]{:S(2)}, u32[]{:S(2)}) collective-permute-start(bf16[2,512,128]{2,1,0:T(8,128)(2,1)} %get-tuple-element.50), channel_id=1, source_target_pairs={{96,0},{112,16},{97,1},{113,17},{98,2},{114,18},{99,3},{115,19},{1... | collective-permute-start | bytes 786440 | tf_op jit(solution)/shard_map/ppermute | solution.py:287
  86.8 1.4 %copy-start.4 = (bf16[2,1024,128]{2,1,0:T(8,128)(2,1)S(1)}, bf16[2,1024,128]{2,1,0:T(8,128)(2,1)}, u32[]{:S(2)}) copy-start(bf16[2,1024,128]{2,1,0:T(8,128)(2,1)} %get-tuple-element.28) | copy-start | bytes 1572868
  87.8 6.9 %collective-permute-start.19 = (bf16[64,2560]{1,0:T(8,128)(2,1)S(1)}, bf16[64,2560]{1,0:T(8,128)(2,1)S(1)}, u32[]{:S(2)}, u32[]{:S(2)}) collective-permute-start(bf16[64,2560]{1,0:T(8,128)(2,1)S(1)} %dynamic-slice_convert_fusion), channel_id=1, source_target_pairs={{0,1},{1,0},{2,3},{3,2},{4,5},{5,4},{6,7},{7,6},{8,9},{9,8},{10,11... | collective-permute-start | bytes 983048 | tf_op jit(solution)/shard_map/ppermute | solution.py:369
  88.2 3.8 %copy-start.5 = (bf16[2,512,128]{2,1,0:T(8,128)(2,1)S(1)}, bf16[2,512,128]{2,1,0:T(8,128)(2,1)}, u32[]{:S(2)}) copy-start(bf16[2,512,128]{2,1,0:T(8,128)(2,1)} %get-tuple-element.47) | copy-start | bytes 786436
  92.2 6.9 %collective-permute-start.18 = (bf16[2,2,128,128]{3,2,1,0:T(8,128)(2,1)S(1)}, bf16[2,2,128,128]{3,2,1,0:T(8,128)(2,1)S(1)}, u32[]{:S(2)}, u32[]{:S(2)}) collective-permute-start(bf16[2,2,128,128]{3,2,1,0:T(8,128)(2,1)S(1)} %slice_bitcast_fusion.6), channel_id=1, source_target_pairs={{0,16},{16,0},{32,48},{48,32},{64,80},{80,64},{96,112},{112,96},{1... | collective-permute-start | bytes 393224 | tf_op jit(solution)/shard_map/ppermute | solution.py:279

commit v3 on v2

--- a/solution.py
+++ b/solution.py
@@ -342,11 +342,12 @@
     middle = zs // 2
     terms[1], dkv[middle] = lax.optimization_barrier((terms[1], dkv[middle]))
     early = shift(dkv.pop(middle), -middle, False)
+    terms[2], dkv[-1] = lax.optimization_barrier((terms[2], dkv[-1]))
     *terms, dq_got = lax.optimization_barrier((*terms, dq_got))
     terms = [x.astype(F32) for x in terms]
     while len(terms) > 1:
         terms = [terms[i] + terms[i + 1] for i in range(0, len(terms), 2)]
-    share, *dkv[1:] = lax.optimization_barrier((terms[0].astype(BF16), *dkv[1:]))
+    share, dkv[1] = lax.optimization_barrier((terms[0].astype(BF16), dkv[1]))
     low = share.reshape(2, 2, prows, width)
     low_got, early = lax.optimization_barrier((swap(low[:, 1]), early))
     low = jnp.concatenate(in_order(low[:, 0], low_got), 2)

time: 102 us -> 103 us (level); the launches traced: 101 us -> 104 us
  waiting for transfers between devices: 25.2 us -> 29.6 us
    ppermute x9, starting transfers between devices: 17.8 us -> 22.8 us  [shift(): return lax.ppermute(x, 'prefix', pairs)]
    ppermute x4, starting transfers between devices: 11.7 us -> 6.79 us  [exchange(): return lax.ppermute(x, 'group', [(i, i ^ step) for i in range(group_size)])]
    ppermute x9, waiting for transfers between devices: 14.7 us -> 16.9 us  [shift(): return lax.ppermute(x, 'prefix', pairs)]
    ppermute x6, waiting for transfers between devices: 6.43 us -> 7.83 us  [swap(): return lax.ppermute(x, 'prefix', [(i, i ^ 1) for i in range(prefix_size)])]
    ppermute x4, waiting for transfers between devices: 2.63 us -> 4 us  [exchange(): return lax.ppermute(x, 'group', [(i, i ^ step) for i in range(group_size)])]
  transfers between devices with their start and end apart: 20 -> 20, of which waited for: 11 -> 12; matrix products, arithmetic and copies ran while one was open for 14% -> 13% of each run, Pallas kernels for 0% -> 0%
where the time goes in v3:
time: 103 us; the launch traced here: 104 us
  starting transfers between devices  38.2 us (37%)
  waiting for transfers between devices  29.6 us (29%)
  Pallas kernels  15.1 us (15%)
  local copies, waits for them, and re-layouts  11.2 us (11%)
  other arithmetic  4.75 us (5%)
  between operations  3.54 us (3%)
  matrix products  1.82 us (2%)
    ppermute x9, starting transfers between devices, shift(): return lax.ppermute(x, 'prefix', pairs)  22.8 us
    ppermute x9, waiting for transfers between devices, shift(): return lax.ppermute(x, 'prefix', pairs)  16.9 us
    pallas_call x1, Pallas kernels, attention(): pl.pallas_call(functools.partial(attention_kernel, tokens, prows, zs, cou...  15.1 us
    ppermute x6, starting transfers between devices, swap(): return lax.ppermute(x, 'prefix', [(i, i ^ 1) for i in range(prefix_size)])  8.23 us
    ppermute x6, waiting for transfers between devices, swap(): return lax.ppermute(x, 'prefix', [(i, i ^ 1) for i in range(prefix_size)])  7.83 us
    ppermute x4, starting transfers between devices, exchange(): return lax.ppermute(x, 'group', [(i, i ^ step) for i in range(group_size)])  6.79 us
    ppermute x4, waiting for transfers between devices, exchange(): return lax.ppermute(x, 'group', [(i, i ^ step) for i in range(group_size)])  4 us
    transpose x2, local copies, waits for them, and re-layouts, per_device(): own = own.transpose(0, 2, 1, 3).reshape(2, factor * tokens, width)  3.88 us
  transfers between devices with their start and end apart: 20, of which 12 were waited for; matrix products, arithmetic and copies ran while one was open for 13% of the time, Pallas kernels for 0%

profile of v3, /device:TPU:1, one launch (start us, length us, event | category | flops | bytes accessed | tf_op | source)
XLA Modules:
  0.0 104.2 jit_solution(1756113220910872408)
XLA Ops:
  0.7 1.2 %copy_bitcast_fusion = (bf16[1,128,2,2,128]{4,1,0,2,3:T(8,128)(2,1)S(1)}, bf16[1,128,2,2,128]{4,1,0,2,3:T(8,128)(2,1)S(1)}) fusion(bf16[128,2,2,128]{3,2,1,0:T(2,128)(2,1)} %param.11, bf16[128,2,2,128]{3,2,1,0:T(2,128)(2,1)} %param.10), kind=kLoop, calls=%fused_computation.32 | loop fusion | bytes 524288 | tf_op jit(solution)/shard_map/stack | solution.py:295
  1.9 0.9 copy_bitcast_fusion.2
  2.8 3.7 %collective-permute-start.2 = (bf16[640,128]{1,0:T(8,128)(2,1)S(1)}, bf16[640,128]{1,0:T(8,128)(2,1)S(1)}, u32[]{:S(2)}, u32[]{:S(2)}) collective-permute-start(bf16[640,128]{1,0:T(8,128)(2,1)S(1)} %pad_maximum_fusion.4), channel_id=1, source_target_pairs={{0,16},{16,0},{32,48},{48,32},{64,80},{80,64},{96,112},{112,96},{1... | collective-permute-start | bytes 491528 | tf_op jit(solution)/shard_map/ppermute | solution.py:279
  6.5 0.2 slice_bitcast_fusion.1
  6.7 0.2 slice_bitcast_fusion
  6.9 1.5 %select_bitcast_fusion = (bf16[2,8,128,128]{3,1,2,0:T(8,128)(2,1)S(1)}, bf16[2,8,128,128]{3,1,2,0:T(8,128)(2,1)}, bf16[2,8,128,128]{3,1,2,0:T(8,128)(2,1)}, bf16[2,8,128,128]{3,1,2,0:T(8,128)(2,1)S(1)}) fusion(pred[]{:T(512)S(6)} %eq.5, bf16[1,128,16,128]{3,2,1,0:T(8,128)(2,1)S(1)} %get-tuple-element.64, bf16[1,128,16,128]{3,2,1,0:T(8,128)(2,1)S(1)} %get-tuple-element.62, ...), kind=kLoop, calls=%fused_computation.13 | loop fusion | flops 7340032 | bytes 4194305 | tf_op jit(solution)/shard_map/transpose | solution.py:319
  8.3 0.9 copy.31
  9.3 0.9 copy.34
  10.1 2.9 %collective-permute-start.1 = (bf16[2,1024,128]{2,1,0:T(8,128)(2,1)}, bf16[2,1024,128]{2,1,0:T(8,128)(2,1)}, u32[]{:S(2)}, u32[]{:S(2)}) collective-permute-start(bf16[2,1024,128]{2,1,0:T(8,128)(2,1)} %bitcast.19), channel_id=1, source_target_pairs={{0,16},{16,0},{32,48},{48,32},{64,80},{80,64},{96,112},{112,96},{1... | collective-permute-start | bytes 1572872 | tf_op jit(solution)/shard_map/ppermute | solution.py:279
  13.2 1.7 %collective-permute-start.3 = (bf16[1280,128]{1,0:T(8,128)(2,1)S(1)}, bf16[1280,128]{1,0:T(8,128)(2,1)S(1)}, u32[]{:S(2)}, u32[]{:S(2)}) collective-permute-start(bf16[1280,128]{1,0:T(8,128)(2,1)S(1)} %pad_maximum_fusion.2.refs_4_), channel_id=1, source_target_pairs={{0,32},{16,48},{32,64},{48,80},{64,96},{80,112},{96,0},{112,16},{1... | collective-permute-start | bytes 983048 | tf_op jit(solution)/shard_map/ppermute | solution.py:287
  15.0 3.3 %collective-permute-start.4 = (bf16[1280,128]{1,0:T(8,128)(2,1)S(1)}, bf16[1280,128]{1,0:T(8,128)(2,1)}, u32[]{:S(2)}, u32[]{:S(2)}) collective-permute-start(bf16[1280,128]{1,0:T(8,128)(2,1)S(1)} %pad_maximum_fusion.2.refs_4_), channel_id=1, source_target_pairs={{0,64},{16,80},{32,96},{48,112},{64,0},{80,16},{96,32},{112,48},{1... | collective-permute-start | bytes 983048 | tf_op jit(solution)/shard_map/ppermute | solution.py:287
  18.3 0.7 collective-permute-start.5
  19.1 0.6 fusion.11
  22.2 1.9 %copy.30 = bf16[2,8,128,128]{3,2,1,0:T(8,128)(2,1)} copy(bf16[2,8,128,128]{3,1,2,0:T(8,128)(2,1)} %get-tuple-element.80) | data formatting | bytes 1048576 | tf_op jit(solution)/shard_map/transpose | solution.py:318
  24.1 1.9 %copy.33 = bf16[2,8,128,128]{3,2,1,0:T(8,128)(2,1)} copy(bf16[2,8,128,128]{3,1,2,0:T(8,128)(2,1)} %get-tuple-element.61) | data formatting | bytes 1048576 | tf_op jit(solution)/shard_map/transpose | solution.py:318
  26.2 5.4 %collective-permute-done.4.refs_6_ = bf16[1280,128]{1,0:T(8,128)(2,1)} collective-permute-done((bf16[1280,128]{1,0:T(8,128)(2,1)S(1)}, bf16[1280,128]{1,0:T(8,128)(2,1)}, u32[]{:S(2)}, u32[]{:S(2)}) %collective-permute-start.4) | collective-permute-done | bytes 327712 | tf_op jit(solution)/shard_map/ppermute | solution.py:287
  31.6 0.3 collective-permute-done.5.refs_7_
  31.9 2.8 %collective-permute-done.1.refs_3_ = bf16[2,1024,128]{2,1,0:T(8,128)(2,1)} collective-permute-done((bf16[2,1024,128]{2,1,0:T(8,128)(2,1)}, bf16[2,1024,128]{2,1,0:T(8,128)(2,1)}, u32[]{:S(2)}, u32[]{:S(2)}) %collective-permute-start.1) | collective-permute-done | bytes 524320 | tf_op jit(solution)/shard_map/ppermute | solution.py:279
  34.8 15.1 %attention_grad.1 = (bf16[2,1024,128]{2,1,0:T(8,128)(2,1)}, bf16[2,1024,128]{2,1,0:T(8,128)(2,1)}, bf16[2,512,128]{2,1,0:T(8,128)(2,1)}, bf16[2,512,128]{2,1,0:T...) custom-call(s32[6]{0:T(128)S(1)} %stack.68.meta, ...), custom_call_target="tpu_custom_call" | custom-call | flops 8053063680 | bytes 8388608 | tf_op jit(solution)/shard_map/attention_grad/pallas_call | solution.py:240
  49.9 2.3 %collective-permute-start.6 = (bf16[256,128]{1,0:T(8,128)(2,1)}, bf16[256,128]{1,0:T(8,128)(2,1)S(1)}, u32[]{:S(2)}, u32[]{:S(2)}) collective-permute-start(bf16[256,128]{1,0:T(8,128)(2,1)} %get-tuple-element.31), channel_id=1, source_target_pairs={{0,96},{16,112},{32,0},{48,16},{64,32},{80,48},{96,64},{112,80},{1... | collective-permute-start | bytes 196616 | tf_op jit(solution)/shard_map/ppermute | solution.py:287
  52.2 9.8 %collective-permute-start.7 = (bf16[256,128]{1,0:T(8,128)(2,1)}, bf16[256,128]{1,0:T(8,128)(2,1)S(1)}, u32[]{:S(2)}, u32[]{:S(2)}) collective-permute-start(bf16[256,128]{1,0:T(8,128)(2,1)} %get-tuple-element.32), channel_id=1, source_target_pairs={{0,64},{16,80},{32,96},{48,112},{64,0},{80,16},{96,32},{112,48},{1... | collective-permute-start | bytes 196616 | tf_op jit(solution)/shard_map/ppermute | solution.py:287
  62.0 0.8 collective-permute-start.8
  62.8 0.9 collective-permute-start.13
  63.7 0.5 collective-permute-done.7
  64.2 2.4 %collective-permute-done.8 = bf16[256,128]{1,0:T(8,128)(2,1)S(1)} collective-permute-done((bf16[256,128]{1,0:T(8,128)(2,1)}, bf16[256,128]{1,0:T(8,128)(2,1)S(1)}, u32[]{:S(2)}, u32[]{:S(2)}) %collective-permute-start.8) | collective-permute-done | bytes 65568 | tf_op jit(solution)/shard_map/ppermute | solution.py:287
  66.6 0.9 convert_add_fusion
  67.5 1.3 %collective-permute-done.9 = f32[256,128]{1,0:T(8,128)S(1)} collective-permute-done((f32[256,128]{1,0:T(8,128)S(1)}, f32[256,128]{1,0:T(8,128)S(1)}, u32[]{:S(2)}, u32[]{:S(2)}) %collective-permute-start.9) | collective-permute-done | bytes 131104 | tf_op jit(solution)/shard_map/ppermute | solution.py:334
  68.9 1.8 %collective-permute-start.11 = (bf16[256,128]{1,0:T(8,128)(2,1)S(1)}, bf16[256,128]{1,0:T(8,128)(2,1)S(1)}, u32[]{:S(2)}, u32[]{:S(2)}) collective-permute-start(bf16[256,128]{1,0:T(8,128)(2,1)S(1)} %add_convert_fusion.3), channel_id=1, source_target_pairs={{0,8},{2,10},{4,12},{6,14},{8,0},{10,2},{12,4},{14,6},{1,9},{3,11}... | collective-permute-start | bytes 196616 | tf_op jit(solution)/shard_map/ppermute | solution.py:334
  70.7 4.6 %collective-permute-start.10 = (bf16[256,128]{1,0:T(8,128)(2,1)S(1)}, bf16[256,128]{1,0:T(8,128)(2,1)S(1)}, u32[]{:S(2)}, u32[]{:S(2)}) collective-permute-start(bf16[256,128]{1,0:T(8,128)(2,1)S(1)} %add_convert_fusion.3), channel_id=1, source_target_pairs={{0,4},{2,6},{4,0},{6,2},{8,12},{10,14},{12,8},{14,10},{1,5},{3,7},... | collective-permute-start | bytes 196616 | tf_op jit(solution)/shard_map/ppermute | solution.py:334
  75.2 0.4 collective-permute-start.12
  75.6 2.6 %collective-permute-done.10 = bf16[256,128]{1,0:T(8,128)(2,1)S(1)} collective-permute-done((bf16[256,128]{1,0:T(8,128)(2,1)S(1)}, bf16[256,128]{1,0:T(8,128)(2,1)S(1)}, u32[]{:S(2)}, u32[]{:S(2)}) %collective-permute-start.10) | collective-permute-done | bytes 65568 | tf_op jit(solution)/shard_map/ppermute | solution.py:334
  78.2 1.3 %collective-permute-start.15 = (bf16[2,512,128]{2,1,0:T(8,128)(2,1)}, bf16[2,512,128]{2,1,0:T(8,128)(2,1)S(1)}, u32[]{:S(2)}, u32[]{:S(2)}) collective-permute-start(bf16[2,512,128]{2,1,0:T(8,128)(2,1)} %get-tuple-element.45), channel_id=1, source_target_pairs={{64,0},{80,16},{96,32},{112,48},{65,1},{81,17},{97,33},{113,49},{6... | collective-permute-start | bytes 786440 | tf_op jit(solution)/shard_map/ppermute | solution.py:287
  79.6 0.6 collective-permute-start.14
  80.2 1.5 %collective-permute-start.17 = (bf16[2,512,128]{2,1,0:T(8,128)(2,1)}, bf16[2,512,128]{2,1,0:T(8,128)(2,1)S(1)}, u32[]{:S(2)}, u32[]{:S(2)}) collective-permute-start(bf16[2,512,128]{2,1,0:T(8,128)(2,1)} %get-tuple-element.52), channel_id=1, source_target_pairs={{96,0},{112,16},{97,1},{113,17},{98,2},{114,18},{99,3},{115,19},{1... | collective-permute-start | bytes 786440 | tf_op jit(solution)/shard_map/ppermute | solution.py:287
  81.8 1.3 %collective-permute-start.16 = (bf16[2,512,128]{2,1,0:T(8,128)(2,1)}, bf16[2,512,128]{2,1,0:T(8,128)(2,1)S(1)}, u32[]{:S(2)}, u32[]{:S(2)}) collective-permute-start(bf16[2,512,128]{2,1,0:T(8,128)(2,1)} %get-tuple-element.51), channel_id=1, source_target_pairs={{32,0},{48,16},{64,32},{80,48},{96,64},{112,80},{33,1},{49,17},{65... | collective-permute-start | bytes 786440 | tf_op jit(solution)/shard_map/ppermute | solution.py:287
  83.1 5.0 %collective-permute-done.15 = bf16[2,512,128]{2,1,0:T(8,128)(2,1)S(1)} collective-permute-done((bf16[2,512,128]{2,1,0:T(8,128)(2,1)}, bf16[2,512,128]{2,1,0:T(8,128)(2,1)S(1)}, u32[]{:S(2)}, u32[]{:S(2)}) %collective-permute-start.15) | collective-permute-done | bytes 262176 | tf_op jit(solution)/shard_map/ppermute | solution.py:287
  88.1 0.9 fusion.4
  89.1 0.9 convolution_add_fusion
  90.0 0.4 collective-permute-start.19
  90.5 0.3 copy.42
  90.8 0.3 copy.43
  91.2 1.2 %maximum_bitcast_fusion = bf16[128,2,16,128]{3,2,1,0:T(8,128)(2,1)} fusion(bf16[2,8,128,128]{3,1,0,2:T(8,128)(2,1)S(1)} %copy.43, bf16[2,8,128,128]{3,1,0,2:T(8,128)(2,1)S(1)} %copy.42), kind=kLoop, calls=%fused_computation.5 | loop fusion | flops 2097152 | bytes 2097152 | tf_op jit(solution)/shard_map/transpose | solution.py:369
  92.3 3.3 %collective-permute-done.17 = bf16[2,512,128]{2,1,0:T(8,128)(2,1)S(1)} collective-permute-done((bf16[2,512,128]{2,1,0:T(8,128)(2,1)}, bf16[2,512,128]{2,1,0:T(8,128)(2,1)S(1)}, u32[]{:S(2)}, u32[]{:S(2)}) %collective-permute-start.17) | collective-permute-done | bytes 262176 | tf_op jit(solution)/shard_map/ppermute | solution.py:287
  95.9 0.9 collective-permute-done.19
  96.8 0.8 add_convert_fusion
  97.6 5.0 %collective-permute-done.18 = bf16[2,2,128,128]{3,2,1,0:T(8,128)(2,1)S(1)} collective-permute-done((bf16[2,2,128,128]{3,2,1,0:T(8,128)(2,1)S(1)}, bf16[2,2,128,128]{3,2,1,0:T(8,128)(2,1)S(1)}, u32[]{:S(2)}, u32[]{:S(2)}) %collective-permute-start.18) | collective-permute-done | bytes 131104 | tf_op jit(solution)/shard_map/ppermute | solution.py:279
  102.7 0.8 copy.46
  103.5 0.8 copy.47
  (51 shorter events, 1.1 us)
Async XLA Ops:
  0.6 87.5 %copy-start = (bf16[5120,256]{1,0:T(8,128)(2,1)S(1)}, bf16[5120,256]{1,0:T(8,128)(2,1)}, u32[]{:S(2)}) copy-start(bf16[5120,256]{1,0:T(8,128)(2,1)} %param.15) | copy-start | bytes 7864324
  0.7 5.8 %copy-start.2 = (bf16[128,2,16,128]{3,2,1,0:T(8,128)(2,1)S(1)}, bf16[128,2,16,128]{3,2,1,0:T(8,128)(2,1)}, u32[]{:S(2)}) copy-start(bf16[128,2,16,128]{3,2,1,0:T(8,128)(2,1)} %param.9) | copy-start | bytes 3145732
  0.7 6.0 %copy-start.3 = (bf16[128,2,16,128]{3,2,1,0:T(8,128)(2,1)S(1)}, bf16[128,2,16,128]{3,2,1,0:T(8,128)(2,1)}, u32[]{:S(2)}) copy-start(bf16[128,2,16,128]{3,2,1,0:T(8,128)(2,1)} %param.12) | copy-start | bytes 3145732
  2.8 10.3 %collective-permute-start.2 = (bf16[640,128]{1,0:T(8,128)(2,1)S(1)}, bf16[640,128]{1,0:T(8,128)(2,1)S(1)}, u32[]{:S(2)}, u32[]{:S(2)}) collective-permute-start(bf16[640,128]{1,0:T(8,128)(2,1)S(1)} %pad_maximum_fusion.4), channel_id=1, source_target_pairs={{0,16},{16,0},{32,48},{48,32},{64,80},{80,64},{96,112},{112,96},{1... | collective-permute-start | bytes 491528 | tf_op jit(solution)/shard_map/ppermute | solution.py:279
  8.3 10.7 %copy-start.6 = (s32[16]{0:T(128)S(1)}, s32[16]{0:T(128)}, u32[]{:S(2)}) copy-start(s32[16]{0:T(128)} %param.17) | copy-start | bytes 196
  9.2 22.7 %collective-permute-start = (bf16[2,1024,128]{2,1,0:T(8,128)(2,1)}, bf16[2,1024,128]{2,1,0:T(8,128)(2,1)}, u32[]{:S(2)}, u32[]{:S(2)}) collective-permute-start(bf16[2,1024,128]{2,1,0:T(8,128)(2,1)} %bitcast.13), channel_id=1, source_target_pairs={{0,16},{16,0},{32,48},{48,32},{64,80},{80,64},{96,112},{112,96},{1... | collective-permute-start | bytes 1572872 | tf_op jit(solution)/shard_map/ppermute | solution.py:279
  10.1 24.6 %collective-permute-start.1 = (bf16[2,1024,128]{2,1,0:T(8,128)(2,1)}, bf16[2,1024,128]{2,1,0:T(8,128)(2,1)}, u32[]{:S(2)}, u32[]{:S(2)}) collective-permute-start(bf16[2,1024,128]{2,1,0:T(8,128)(2,1)} %bitcast.19), channel_id=1, source_target_pairs={{0,16},{16,0},{32,48},{48,32},{64,80},{80,64},{96,112},{112,96},{1... | collective-permute-start | bytes 1572872 | tf_op jit(solution)/shard_map/ppermute | solution.py:279
  13.2 12.9 %collective-permute-start.3 = (bf16[1280,128]{1,0:T(8,128)(2,1)S(1)}, bf16[1280,128]{1,0:T(8,128)(2,1)S(1)}, u32[]{:S(2)}, u32[]{:S(2)}) collective-permute-start(bf16[1280,128]{1,0:T(8,128)(2,1)S(1)} %pad_maximum_fusion.2.refs_4_), channel_id=1, source_target_pairs={{0,32},{16,48},{32,64},{48,80},{64,96},{80,112},{96,0},{112,16},{1... | collective-permute-start | bytes 983048 | tf_op jit(solution)/shard_map/ppermute | solution.py:287
  15.0 16.6 %collective-permute-start.4 = (bf16[1280,128]{1,0:T(8,128)(2,1)S(1)}, bf16[1280,128]{1,0:T(8,128)(2,1)}, u32[]{:S(2)}, u32[]{:S(2)}) collective-permute-start(bf16[1280,128]{1,0:T(8,128)(2,1)S(1)} %pad_maximum_fusion.2.refs_4_), channel_id=1, source_target_pairs={{0,64},{16,80},{32,96},{48,112},{64,0},{80,16},{96,32},{112,48},{1... | collective-permute-start | bytes 983048 | tf_op jit(solution)/shard_map/ppermute | solution.py:287
  18.3 13.7 %collective-permute-start.5 = (bf16[1280,128]{1,0:T(8,128)(2,1)S(1)}, bf16[1280,128]{1,0:T(8,128)(2,1)}, u32[]{:S(2)}, u32[]{:S(2)}) collective-permute-start(bf16[1280,128]{1,0:T(8,128)(2,1)S(1)} %pad_maximum_fusion.2.refs_4_), channel_id=1, source_target_pairs={{0,96},{16,112},{32,0},{48,16},{64,32},{80,48},{96,64},{112,80},{1... | collective-permute-start | bytes 983048 | tf_op jit(solution)/shard_map/ppermute | solution.py:287
  49.9 13.8 %collective-permute-start.6 = (bf16[256,128]{1,0:T(8,128)(2,1)}, bf16[256,128]{1,0:T(8,128)(2,1)S(1)}, u32[]{:S(2)}, u32[]{:S(2)}) collective-permute-start(bf16[256,128]{1,0:T(8,128)(2,1)} %get-tuple-element.31), channel_id=1, source_target_pairs={{0,96},{16,112},{32,0},{48,16},{64,32},{80,48},{96,64},{112,80},{1... | collective-permute-start | bytes 196616 | tf_op jit(solution)/shard_map/ppermute | solution.py:287
  52.2 12.0 %collective-permute-start.7 = (bf16[256,128]{1,0:T(8,128)(2,1)}, bf16[256,128]{1,0:T(8,128)(2,1)S(1)}, u32[]{:S(2)}, u32[]{:S(2)}) collective-permute-start(bf16[256,128]{1,0:T(8,128)(2,1)} %get-tuple-element.32), channel_id=1, source_target_pairs={{0,64},{16,80},{32,96},{48,112},{64,0},{80,16},{96,32},{112,48},{1... | collective-permute-start | bytes 196616 | tf_op jit(solution)/shard_map/ppermute | solution.py:287
  62.0 4.5 %collective-permute-start.8 = (bf16[256,128]{1,0:T(8,128)(2,1)}, bf16[256,128]{1,0:T(8,128)(2,1)S(1)}, u32[]{:S(2)}, u32[]{:S(2)}) collective-permute-start(bf16[256,128]{1,0:T(8,128)(2,1)} %get-tuple-element.33), channel_id=1, source_target_pairs={{0,32},{16,48},{32,64},{48,80},{64,96},{80,112},{96,0},{112,16},{1... | collective-permute-start | bytes 196616 | tf_op jit(solution)/shard_map/ppermute | solution.py:287
  62.8 16.8 %collective-permute-start.13 = (bf16[2,1024,128]{2,1,0:T(8,128)(2,1)}, bf16[2,1024,128]{2,1,0:T(8,128)(2,1)S(1)}, u32[]{:S(2)}, u32[]{:S(2)}) collective-permute-start(bf16[2,1024,128]{2,1,0:T(8,128)(2,1)} %get-tuple-element.38), channel_id=1, source_target_pairs={{0,16},{16,0},{32,48},{48,32},{64,80},{80,64},{96,112},{112,96},{1... | collective-permute-start | bytes 1572872 | tf_op jit(solution)/shard_map/ppermute | solution.py:279
  67.4 1.4 %collective-permute-start.9 = (f32[256,128]{1,0:T(8,128)S(1)}, f32[256,128]{1,0:T(8,128)S(1)}, u32[]{:S(2)}, u32[]{:S(2)}) collective-permute-start(f32[256,128]{1,0:T(8,128)S(1)} %convert_add_fusion), channel_id=1, source_target_pairs={{0,2},{2,0},{4,6},{6,4},{8,10},{10,8},{12,14},{14,12},{1,3},{3,1},... | collective-permute-start | bytes 393224 | tf_op jit(solution)/shard_map/ppermute | solution.py:334
  68.9 6.7 %collective-permute-start.11 = (bf16[256,128]{1,0:T(8,128)(2,1)S(1)}, bf16[256,128]{1,0:T(8,128)(2,1)S(1)}, u32[]{:S(2)}, u32[]{:S(2)}) collective-permute-start(bf16[256,128]{1,0:T(8,128)(2,1)S(1)} %add_convert_fusion.3), channel_id=1, source_target_pairs={{0,8},{2,10},{4,12},{6,14},{8,0},{10,2},{12,4},{14,6},{1,9},{3,11}... | collective-permute-start | bytes 196616 | tf_op jit(solution)/shard_map/ppermute | solution.py:334
  70.7 7.5 %collective-permute-start.10 = (bf16[256,128]{1,0:T(8,128)(2,1)S(1)}, bf16[256,128]{1,0:T(8,128)(2,1)S(1)}, u32[]{:S(2)}, u32[]{:S(2)}) collective-permute-start(bf16[256,128]{1,0:T(8,128)(2,1)S(1)} %add_convert_fusion.3), channel_id=1, source_target_pairs={{0,4},{2,6},{4,0},{6,2},{8,12},{10,14},{12,8},{14,10},{1,5},{3,7},... | collective-permute-start | bytes 196616 | tf_op jit(solution)/shard_map/ppermute | solution.py:334
  75.2 4.3 %collective-permute-start.12 = (bf16[256,128]{1,0:T(8,128)(2,1)S(1)}, bf16[256,128]{1,0:T(8,128)(2,1)S(1)}, u32[]{:S(2)}, u32[]{:S(2)}) collective-permute-start(bf16[256,128]{1,0:T(8,128)(2,1)S(1)} %add_convert_fusion.3), channel_id=1, source_target_pairs={{0,12},{2,14},{4,8},{6,10},{8,4},{10,6},{12,0},{14,2},{1,13},{3,15... | collective-permute-start | bytes 196616 | tf_op jit(solution)/shard_map/ppermute | solution.py:334
  78.2 9.9 %collective-permute-start.15 = (bf16[2,512,128]{2,1,0:T(8,128)(2,1)}, bf16[2,512,128]{2,1,0:T(8,128)(2,1)S(1)}, u32[]{:S(2)}, u32[]{:S(2)}) collective-permute-start(bf16[2,512,128]{2,1,0:T(8,128)(2,1)} %get-tuple-element.45), channel_id=1, source_target_pairs={{64,0},{80,16},{96,32},{112,48},{65,1},{81,17},{97,33},{113,49},{6... | collective-permute-start | bytes 786440 | tf_op jit(solution)/shard_map/ppermute | solution.py:287
  79.6 8.5 %collective-permute-start.14 = (bf16[2,64,128]{2,1,0:T(8,128)(2,1)S(1)}, bf16[2,64,128]{2,1,0:T(8,128)(2,1)S(1)}, u32[]{:S(2)}, u32[]{:S(2)}) collective-permute-start(bf16[2,64,128]{2,1,0:T(8,128)(2,1)S(1)} %slice_bitcast_fusion.8), channel_id=1, source_target_pairs={{0,16},{16,0},{32,48},{48,32},{64,80},{80,64},{96,112},{112,96},{1... | collective-permute-start | bytes 98312 | tf_op jit(solution)/shard_map/ppermute | solution.py:279
  80.2 8.8 %copy-start.1 = (bf16[5120,256]{1,0:T(8,128)(2,1)S(1)}, bf16[5120,256]{1,0:T(8,128)(2,1)}, u32[]{:S(2)}) copy-start(bf16[5120,256]{1,0:T(8,128)(2,1)} %param.16) | copy-start | bytes 7864324
  80.2 15.4 %collective-permute-start.17 = (bf16[2,512,128]{2,1,0:T(8,128)(2,1)}, bf16[2,512,128]{2,1,0:T(8,128)(2,1)S(1)}, u32[]{:S(2)}, u32[]{:S(2)}) collective-permute-start(bf16[2,512,128]{2,1,0:T(8,128)(2,1)} %get-tuple-element.52), channel_id=1, source_target_pairs={{96,0},{112,16},{97,1},{113,17},{98,2},{114,18},{99,3},{115,19},{1... | collective-permute-start | bytes 786440 | tf_op jit(solution)/shard_map/ppermute | solution.py:287
  81.8 13.8 %collective-permute-start.16 = (bf16[2,512,128]{2,1,0:T(8,128)(2,1)}, bf16[2,512,128]{2,1,0:T(8,128)(2,1)S(1)}, u32[]{:S(2)}, u32[]{:S(2)}) collective-permute-start(bf16[2,512,128]{2,1,0:T(8,128)(2,1)} %get-tuple-element.51), channel_id=1, source_target_pairs={{32,0},{48,16},{64,32},{80,48},{96,64},{112,80},{33,1},{49,17},{65... | collective-permute-start | bytes 786440 | tf_op jit(solution)/shard_map/ppermute | solution.py:287
  89.0 1.4 %copy-start.4 = (bf16[2,1024,128]{2,1,0:T(8,128)(2,1)S(1)}, bf16[2,1024,128]{2,1,0:T(8,128)(2,1)}, u32[]{:S(2)}) copy-start(bf16[2,1024,128]{2,1,0:T(8,128)(2,1)} %get-tuple-element.29) | copy-start | bytes 1572868
  90.0 6.8 %collective-permute-start.19 = (bf16[64,2560]{1,0:T(8,128)(2,1)S(1)}, bf16[64,2560]{1,0:T(8,128)(2,1)S(1)}, u32[]{:S(2)}, u32[]{:S(2)}) collective-permute-start(bf16[64,2560]{1,0:T(8,128)(2,1)S(1)} %dynamic-slice_convert_fusion), channel_id=1, source_target_pairs={{0,1},{1,0},{2,3},{3,2},{4,5},{5,4},{6,7},{7,6},{8,9},{9,8},{10,11... | collective-permute-start | bytes 983048 | tf_op jit(solution)/shard_map/ppermute | solution.py:370
  90.5 5.1 %copy-start.5 = (bf16[2,512,128]{2,1,0:T(8,128)(2,1)S(1)}, bf16[2,512,128]{2,1,0:T(8,128)(2,1)}, u32[]{:S(2)}) copy-start(bf16[2,512,128]{2,1,0:T(8,128)(2,1)} %get-tuple-element.49) | copy-start | bytes 786436
  95.8 6.8 %collective-permute-start.18 = (bf16[2,2,128,128]{3,2,1,0:T(8,128)(2,1)S(1)}, bf16[2,2,128,128]{3,2,1,0:T(8,128)(2,1)S(1)}, u32[]{:S(2)}, u32[]{:S(2)}) collective-permute-start(bf16[2,2,128,128]{3,2,1,0:T(8,128)(2,1)S(1)} %slice_bitcast_fusion.6), channel_id=1, source_target_pairs={{0,16},{16,0},{32,48},{48,32},{64,80},{80,64},{96,112},{112,96},{1... | collective-permute-start | bytes 393224 | tf_op jit(solution)/shard_map/ppermute | solution.py:279
